TPU v7x, 32 devices: a whole 2x2x4 slice. The times are simulated.
32 devices in a mesh: seq: 16 (over z, y, x), tp: 2 (over core).
Axes of the slice: x: 2, y: 2, z: 4, core: 2. Of those that a mesh axis runs over, the one named last changes fastest.
Arguments:
- tokens: bfloat16 [128, 16, 2048], P('seq', None, 'tp'), may hold values from -6 to 6
- gain_in: bfloat16 [2048], replicated, may hold values from 0.25 to 1.75
- w_qkv: bfloat16 [3, 2048, 2048], P(None, None, 'tp'), may hold values from -0.125 to 0.125
- w_beta: bfloat16 [2048, 16], P(None, 'tp'), may hold values from -0.25 to 0.25
- conv_weight: bfloat16 [4, 3, 2048], P(None, None, 'tp'), may hold values from -3 to 3
- out_gain: bfloat16 [128], replicated, may hold values from 0.25 to 1.75
- w_out: bfloat16 [2048, 2048], P('tp'), may hold values from -0.125 to 0.125
- state_pages: bfloat16 [128, 16, 128, 128], P('seq', 'tp'), may hold values from -4 to 4
- conv_pages: bfloat16 [128, 3, 3, 2048], P('seq', None, None, 'tp'), may hold values from -6 to 6
- page_order: int32 [128], replicated, may hold values from 0 to 127, as said below
- draft_lengths: int32 [128], replicated, may hold values from 1 to 16
- accepted: int32 [128], replicated, may hold values from 0 to 16
Outputs:
- mixed: bfloat16 [128, 16, 2048], P('seq', None, 'tp')
- final_pages: bfloat16 [128, 16, 128, 128], P('seq', 'tp')
- final_conv: bfloat16 [128, 3, 3, 2048], P('seq', None, None, 'tp')
Inputs may be any that keep to these rules, and one draw needn't show every extreme that they name: page_order is a permutation of all requests; slot s lies on seq device s // 8 and holds a request r of the same device (r // 8) or of one of the two devices next to it along seq, taken cyclically; the slots of one device that hold requests of one neighbour are at most 4, exactly 4 for some pair of devices, and as many as the slots of that neighbour that hold requests of the first device.
All inputs are finite; a program needn't handle non-finite values.
Results may differ from a plain program's by a relative error of at most 0.015.
Values may be sent and summed in bfloat16 or wider, within the bound.
A program may use at most 64 MiB of HBM per device.

v0:
```python
import jax
import jax.numpy as jnp
from jax import lax
from jax.sharding import PartitionSpec as P

D = 2048
DK = 128
CONV = 4
MOVE = 4


def passed_along(array, axis, by):
    count = lax.axis_size(axis)
    return lax.ppermute(array, axis, [(i, (i + by) % count) for i in range(count)])


def rms_rows(values, gain):
    wide = values.astype(jnp.float32)
    return (
        wide
        * lax.rsqrt(jnp.mean(wide * wide, axis=-1, keepdims=True) + 1e-06)
        * gain.astype(jnp.float32)
    )


def unit_heads(values):
    return values * lax.rsqrt(jnp.sum(values * values, axis=-1, keepdims=True) + 1e-06)


def packing(homes, target):
    slot_count = homes.shape[0]
    wanted = homes == target
    ranks = jnp.cumsum(wanted.astype(jnp.int32)) - 1
    table = wanted[None, :] & (ranks[None, :] == jnp.arange(MOVE, dtype=jnp.int32)[:, None])
    positions = jnp.sum(
        table.astype(jnp.int32) * jnp.arange(slot_count, dtype=jnp.int32)[None, :], axis=1
    )
    filled = jnp.any(table, axis=1)
    return (positions, filled)


def select_rows(values, positions, filled):
    rows = jnp.take(values, positions, axis=0)
    shape = (filled.shape[0],) + (1,) * (values.ndim - 1)
    return jnp.where(filled.reshape(shape), rows, jnp.zeros_like(rows))


def slots_of(page_order, device, req_dev):
    return lax.dynamic_slice_in_dim(page_order, device * req_dev, req_dev)


def arriving(page_order, source, place_now, req_dev):
    source_ids = slots_of(page_order, source, req_dev)
    positions, filled = packing(source_ids // req_dev, place_now)
    return jnp.where(filled, jnp.take(source_ids, positions) - place_now * req_dev, -1)


def owned_there(page_order, target, place_now, req_dev):
    target_ids = slots_of(page_order, target, req_dev)
    positions, filled = packing(target_ids // req_dev, place_now)
    rows = jnp.clip(jnp.take(target_ids, positions) - place_now * req_dev, 0, req_dev - 1)
    return (rows, filled)


def collect(buffer, buffer_ids, wanted_count):
    wanted = jnp.arange(wanted_count, dtype=jnp.int32)
    match = buffer_ids[None, :] == wanted[:, None]
    where_at = jnp.sum(
        match.astype(jnp.int32) * jnp.arange(buffer_ids.shape[0], dtype=jnp.int32)[None, :], axis=1
    )
    return jnp.take(buffer, where_at, axis=0)


def place_rows(own_rows, resident, arrivals, homes):
    shape = (homes.shape[0],) + (1,) * (own_rows.ndim - 1)
    final_result = jnp.where(resident.reshape(shape), own_rows, jnp.zeros_like(own_rows))
    for received, source in arrivals:
        wanted = homes == source
        ranks = jnp.clip(jnp.cumsum(wanted.astype(jnp.int32)) - 1, 0, received.shape[0] - 1)
        final_result = jnp.where(
            wanted.reshape(shape), jnp.take(received, ranks, axis=0), final_result
        )
    return final_result


def mix_layer(
    sliced,
    start_pages,
    start_edges,
    lengths,
    kept,
    gain_in,
    w_qkv,
    w_beta,
    conv_weight,
    out_gain,
    w_out,
):
    whole = lax.all_gather(sliced, "tp", axis=2, tiled=True)
    req_count = whole.shape[0]
    drafts = whole.shape[1]
    heads_loc = start_pages.shape[1]
    hidden_loc = heads_loc * DK
    row_count = req_count * drafts
    flat = whole.reshape(row_count, D)
    normed = rms_rows(flat, gain_in).astype(jnp.bfloat16)
    projected = jnp.einsum("rd,cde->rce", normed, w_qkv, preferred_element_type=jnp.float32)
    projected = projected.astype(jnp.bfloat16).reshape(req_count, drafts, 3, hidden_loc)
    extended = jnp.concatenate([start_edges, projected], axis=1)
    summed = jnp.zeros(projected.shape, jnp.float32)
    for offset in range(CONV):
        summed = summed + extended[:, offset : offset + drafts].astype(jnp.float32) * conv_weight[
            offset
        ].astype(jnp.float32)
    active = jax.nn.silu(summed).reshape(req_count, drafts, 3, heads_loc, DK)
    queries = jnp.moveaxis(unit_heads(active[:, :, 0]) * DK ** (-0.5), 1, 0)
    keys_all = jnp.moveaxis(unit_heads(active[:, :, 1]), 1, 0)
    values_all = jnp.moveaxis(active[:, :, 2], 1, 0)
    live = jnp.arange(drafts, dtype=jnp.int32)[None, :] < lengths[:, None]
    rates = jax.nn.sigmoid(jnp.dot(normed, w_beta, preferred_element_type=jnp.float32)).reshape(
        req_count, drafts, heads_loc
    )
    rates = jnp.moveaxis(rates * live[:, :, None].astype(jnp.float32), 1, 0)
    start = start_pages.astype(jnp.float32)

    def advance(carry, inputs):
        state, snapshot = carry
        query, key_t, value, rate, index = inputs
        recalled = jnp.einsum("rhkv,rhk->rhv", state, key_t, precision=lax.Precision.HIGHEST)
        state = state + (rate[..., None] * key_t)[..., :, None] * (value - recalled)[..., None, :]
        output = jnp.einsum("rhkv,rhk->rhv", state, query, precision=lax.Precision.HIGHEST)
        snapshot = jnp.where((kept == index + 1)[:, None, None, None], state, snapshot)
        return ((state, snapshot), output)

    steps_in = (queries, keys_all, values_all, rates, jnp.arange(drafts, dtype=jnp.int32))
    (last_state, snapshot), outputs = lax.scan(advance, (start, start), steps_in)
    normed_out = (
        rms_rows(jnp.moveaxis(outputs, 0, 1), out_gain)
        .astype(jnp.bfloat16)
        .reshape(row_count, hidden_loc)
    )
    columns = sliced.shape[2]
    attended = lax.psum_scatter(
        lax.dot_general(
            w_out, normed_out, (((0,), (1,)), ((), ())), preferred_element_type=jnp.float32
        ).astype(jnp.bfloat16),
        "tp",
        scatter_dimension=0,
        tiled=True,
    ).astype(jnp.float32)
    mixed = (sliced.reshape(row_count, columns).astype(jnp.float32) + attended.T).astype(
        jnp.bfloat16
    )
    mixed = mixed.reshape(req_count, drafts, columns)
    mixed = jnp.where(live[:, :, None], mixed, jnp.zeros_like(mixed))
    picks = kept[:, None] + jnp.arange(CONV - 1, dtype=jnp.int32)[None, :]
    edges = jnp.take_along_axis(extended, picks[:, :, None, None], axis=1)
    return (mixed, snapshot.astype(jnp.bfloat16), edges)


def on_device(
    tokens,
    gain_in,
    w_qkv,
    w_beta,
    conv_weight,
    out_gain,
    w_out,
    state_pages,
    conv_pages,
    page_order,
    draft_lengths,
    accepted,
):
    place_now = lax.axis_index("seq")
    devices_seq = lax.axis_size("seq")
    req_dev = state_pages.shape[0]
    base_row = place_now * req_dev
    own_ids = slots_of(page_order, place_now, req_dev)
    own_homes = own_ids // req_dev
    resident = own_homes == place_now
    local_ids = jnp.where(resident, own_ids - base_row, -1)
    local_rows = jnp.clip(local_ids, 0, req_dev - 1)
    weights = (gain_in, w_qkv, w_beta, conv_weight, out_gain, w_out)
    own_lengths = lax.dynamic_slice_in_dim(draft_lengths, base_row, req_dev)
    own_kept = jnp.minimum(lax.dynamic_slice_in_dim(accepted, base_row, req_dev), own_lengths)
    pool_pages = [state_pages]
    pool_edges = [conv_pages]
    pool_ids = [local_ids]
    for step_by in (1, -1):
        target = (place_now + step_by + devices_seq) % devices_seq
        positions, filled = packing(own_homes, target)
        sending = (
            select_rows(state_pages, positions, filled),
            select_rows(conv_pages, positions, filled),
        )
        got_pages, got_edges = passed_along((sending[0], sending[1]), "seq", step_by)
        source = (place_now - step_by + devices_seq) % devices_seq
        pool_pages.append(got_pages)
        pool_edges.append(got_edges)
        pool_ids.append(arriving(page_order, source, place_now, req_dev))
    all_ids = jnp.concatenate(pool_ids, axis=0)
    start_pages = collect(jnp.concatenate(pool_pages, axis=0), all_ids, req_dev)
    start_edges = collect(jnp.concatenate(pool_edges, axis=0), all_ids, req_dev)
    mixed, final_state, edges = mix_layer(
        tokens, start_pages, start_edges, own_lengths, own_kept, *weights
    )
    page_arrivals = []
    edge_arrivals = []
    for step_by in (1, -1):
        target = (place_now + step_by + devices_seq) % devices_seq
        rows, filled = owned_there(page_order, target, place_now, req_dev)
        sending = (select_rows(final_state, rows, filled), select_rows(edges, rows, filled))
        got_pages, got_edges = passed_along((sending[0], sending[1]), "seq", step_by)
        source = (place_now - step_by + devices_seq) % devices_seq
        page_arrivals.append((got_pages, source))
        edge_arrivals.append((got_edges, source))
    final_pages = place_rows(
        jnp.take(final_state, local_rows, axis=0), resident, page_arrivals, own_homes
    )
    final_conv = place_rows(jnp.take(edges, local_rows, axis=0), resident, edge_arrivals, own_homes)
    return (mixed, final_pages, final_conv)


def solution(mesh):
    return jax.shard_map(
        on_device,
        mesh=mesh,
        in_specs=(
            P("seq", None, "tp"),
            P(),
            P(None, None, "tp"),
            P(None, "tp"),
            P(None, None, "tp"),
            P(),
            P("tp", None),
            P("seq", "tp", None, None),
            P("seq", None, None, "tp"),
            P(),
            P(),
            P(),
        ),
        out_specs=(P("seq", None, "tp"), P("seq", "tp", None, None), P("seq", None, None, "tp")),
        check_vma=False,
    )
```

profile of v0, /device:TPU:0, one launch (start us, length us, event | category | flops | bytes accessed | tf_op | source)
XLA Modules:
  0.0 410.9 jit_solution(8111594958753633548)
XLA Ops:
  11.3 7.0 %collective-permute-start.3 = (bf16[4,3,3,1024]{3,0,2,1:T(4,128)(2,1)S(1)}, bf16[4,3,3,1024]{3,0,2,1:T(4,128)(2,1)S(1)}, u32[]{:S(2)}, u32[]{:S(2)}) collective-permute-start(bf16[4,3,3,1024]{3,0,2,1:T(4,128)(2,1)S(1)} %select_select_fusion.5), channel_id=1, source_target_pairs={{0,30},{2,0},{4,2},{6,4},{8,6},{10,8},{12,10},{14,12},{16,14},{18,... | collective-permute-start | bytes 221192 | tf_op jit(solution)/shard_map/ppermute | solution.py:14
  24.7 5.6 %collective-permute-start.1 = (bf16[4,8,128,128]{3,2,1,0:T(8,128)(2,1)}, bf16[4,8,128,128]{3,2,1,0:T(8,128)(2,1)}, u32[]{:S(2)}, u32[]{:S(2)}) collective-permute-start(bf16[4,8,128,128]{3,2,1,0:T(8,128)(2,1)} %select_select_fusion.3), channel_id=1, source_target_pairs={{0,30},{2,0},{4,2},{6,4},{8,6},{10,8},{12,10},{14,12},{16,14},{18,... | collective-permute-start | bytes 3145736 | tf_op jit(solution)/shard_map/ppermute | solution.py:14
  39.4 6.4 %convolution_convert_fusion.1 = bf16[128,3,1024]{2,0,1:T(8,128)(2,1)S(1)} fusion(bf16[3,2048,1024]{2,1,0:T(8,128)(2,1)} %param.26, bf16[128,2048]{1,0:T(8,128)(2,1)S(1)} %fusion.6), kind=kOutput, calls=%fused_computation.39 | convolution fusion | flops 1611005952 | bytes 13893632 | tf_op jit(solution)/shard_map/rd,cde->rce/dot_general | solution.py:107
  57.8 10.0 %collective-permute-done = bf16[4,8,128,128]{3,2,1,0:T(8,128)(2,1)} collective-permute-done((bf16[4,8,128,128]{3,2,1,0:T(8,128)(2,1)}, bf16[4,8,128,128]{3,2,1,0:T(8,128)(2,1)}, u32[]{:S(2)}, u32[]{:S(2)}) %collective-permute-start) | collective-permute-done | bytes 1048608 | tf_op jit(solution)/shard_map/ppermute | solution.py:14
  76.3 4.4 %fusion.44 = (bf16[8,8,128,128]{3,2,1,0:T(8,128)(2,1)S(1)}, f32[8,8,128,128]{3,2,1,0:T(8,128)}) fusion(bf16[8,8,128,128]{3,2,1,0:T(8,128)(2,1)} %gather_fusion, pred[8]{0:T(512)(128)(4,1)S(1)} %copy-done.34), kind=kLoop, calls=%fused_computation.196 | loop fusion | flops 3145728 | bytes 8388616
  81.1 242.1 %while.14 = (s32[]{:T(128)}, f32[8,8,128,128]{3,2,1,0:T(8,128)}, bf16[8,8,128,128]{3,2,1,0:T(8,128)(2,1)S(1)}, f32[16,8,8,128]{3,2,1,0:T(8,128)S(1)}, f32[16,8,8...) while((s32[]{:T(128)}, f32[8,8,128,128]{3,2,1,0:T(8,128)}, ...), condition=%wide.region_17.21_spmd, body=%wide.region_16.20_spmd.sunk | while | flops 28327948 | bytes 55051284 | solution.py:136
  83.8 5.4 %fusion.68 = f32[8,8,1,128]{3,2,1,0:T(1,128)S(1)} fusion(f32[8,8,128,1]{2,3,1,0:T(1,128)S(1)} %bitcast.164, f32[8,8,128,128]{3,2,1,0:T(8,128)} %get-tuple-element.310), kind=kOutput, calls=%fused_computation.197.clone.1 | convolution fusion | flops 12582912 | bytes 4259840 | tf_op jit(solution)/shard_map/while/body/eval_jaxpr/rhkv,rhk->rhv/dot_general | solution.py:129
  98.9 5.4 %fusion.68 = f32[8,8,1,128]{3,2,1,0:T(1,128)S(1)} fusion(f32[8,8,128,1]{2,3,1,0:T(1,128)S(1)} %bitcast.164, f32[8,8,128,128]{3,2,1,0:T(8,128)} %get-tuple-element.310), kind=kOutput, calls=%fused_computation.197.clone.1 | convolution fusion | flops 12582912 | bytes 4259840 | tf_op jit(solution)/shard_map/while/body/eval_jaxpr/rhkv,rhk->rhv/dot_general | solution.py:129
  114.1 5.4 %fusion.68 = f32[8,8,1,128]{3,2,1,0:T(1,128)S(1)} fusion(f32[8,8,128,1]{2,3,1,0:T(1,128)S(1)} %bitcast.164, f32[8,8,128,128]{3,2,1,0:T(8,128)} %get-tuple-element.310), kind=kOutput, calls=%fused_computation.197.clone.1 | convolution fusion | flops 12582912 | bytes 4259840 | tf_op jit(solution)/shard_map/while/body/eval_jaxpr/rhkv,rhk->rhv/dot_general | solution.py:129
  129.2 5.4 %fusion.68 = f32[8,8,1,128]{3,2,1,0:T(1,128)S(1)} fusion(f32[8,8,128,1]{2,3,1,0:T(1,128)S(1)} %bitcast.164, f32[8,8,128,128]{3,2,1,0:T(8,128)} %get-tuple-element.310), kind=kOutput, calls=%fused_computation.197.clone.1 | convolution fusion | flops 12582912 | bytes 4259840 | tf_op jit(solution)/shard_map/while/body/eval_jaxpr/rhkv,rhk->rhv/dot_general | solution.py:129
  144.3 5.4 %fusion.68 = f32[8,8,1,128]{3,2,1,0:T(1,128)S(1)} fusion(f32[8,8,128,1]{2,3,1,0:T(1,128)S(1)} %bitcast.164, f32[8,8,128,128]{3,2,1,0:T(8,128)} %get-tuple-element.310), kind=kOutput, calls=%fused_computation.197.clone.1 | convolution fusion | flops 12582912 | bytes 4259840 | tf_op jit(solution)/shard_map/while/body/eval_jaxpr/rhkv,rhk->rhv/dot_general | solution.py:129
  159.5 5.4 %fusion.68 = f32[8,8,1,128]{3,2,1,0:T(1,128)S(1)} fusion(f32[8,8,128,1]{2,3,1,0:T(1,128)S(1)} %bitcast.164, f32[8,8,128,128]{3,2,1,0:T(8,128)} %get-tuple-element.310), kind=kOutput, calls=%fused_computation.197.clone.1 | convolution fusion | flops 12582912 | bytes 4259840 | tf_op jit(solution)/shard_map/while/body/eval_jaxpr/rhkv,rhk->rhv/dot_general | solution.py:129
  174.6 5.4 %fusion.68 = f32[8,8,1,128]{3,2,1,0:T(1,128)S(1)} fusion(f32[8,8,128,1]{2,3,1,0:T(1,128)S(1)} %bitcast.164, f32[8,8,128,128]{3,2,1,0:T(8,128)} %get-tuple-element.310), kind=kOutput, calls=%fused_computation.197.clone.1 | convolution fusion | flops 12582912 | bytes 4259840 | tf_op jit(solution)/shard_map/while/body/eval_jaxpr/rhkv,rhk->rhv/dot_general | solution.py:129
  189.7 5.4 %fusion.68 = f32[8,8,1,128]{3,2,1,0:T(1,128)S(1)} fusion(f32[8,8,128,1]{2,3,1,0:T(1,128)S(1)} %bitcast.164, f32[8,8,128,128]{3,2,1,0:T(8,128)} %get-tuple-element.310), kind=kOutput, calls=%fused_computation.197.clone.1 | convolution fusion | flops 12582912 | bytes 4259840 | tf_op jit(solution)/shard_map/while/body/eval_jaxpr/rhkv,rhk->rhv/dot_general | solution.py:129
  204.9 5.4 %fusion.68 = f32[8,8,1,128]{3,2,1,0:T(1,128)S(1)} fusion(f32[8,8,128,1]{2,3,1,0:T(1,128)S(1)} %bitcast.164, f32[8,8,128,128]{3,2,1,0:T(8,128)} %get-tuple-element.310), kind=kOutput, calls=%fused_computation.197.clone.1 | convolution fusion | flops 12582912 | bytes 4259840 | tf_op jit(solution)/shard_map/while/body/eval_jaxpr/rhkv,rhk->rhv/dot_general | solution.py:129
  220.0 5.4 %fusion.68 = f32[8,8,1,128]{3,2,1,0:T(1,128)S(1)} fusion(f32[8,8,128,1]{2,3,1,0:T(1,128)S(1)} %bitcast.164, f32[8,8,128,128]{3,2,1,0:T(8,128)} %get-tuple-element.310), kind=kOutput, calls=%fused_computation.197.clone.1 | convolution fusion | flops 12582912 | bytes 4259840 | tf_op jit(solution)/shard_map/while/body/eval_jaxpr/rhkv,rhk->rhv/dot_general | solution.py:129
  235.1 5.4 %fusion.68 = f32[8,8,1,128]{3,2,1,0:T(1,128)S(1)} fusion(f32[8,8,128,1]{2,3,1,0:T(1,128)S(1)} %bitcast.164, f32[8,8,128,128]{3,2,1,0:T(8,128)} %get-tuple-element.310), kind=kOutput, calls=%fused_computation.197.clone.1 | convolution fusion | flops 12582912 | bytes 4259840 | tf_op jit(solution)/shard_map/while/body/eval_jaxpr/rhkv,rhk->rhv/dot_general | solution.py:129
  250.2 5.4 %fusion.68 = f32[8,8,1,128]{3,2,1,0:T(1,128)S(1)} fusion(f32[8,8,128,1]{2,3,1,0:T(1,128)S(1)} %bitcast.164, f32[8,8,128,128]{3,2,1,0:T(8,128)} %get-tuple-element.310), kind=kOutput, calls=%fused_computation.197.clone.1 | convolution fusion | flops 12582912 | bytes 4259840 | tf_op jit(solution)/shard_map/while/body/eval_jaxpr/rhkv,rhk->rhv/dot_general | solution.py:129
  265.4 5.4 %fusion.68 = f32[8,8,1,128]{3,2,1,0:T(1,128)S(1)} fusion(f32[8,8,128,1]{2,3,1,0:T(1,128)S(1)} %bitcast.164, f32[8,8,128,128]{3,2,1,0:T(8,128)} %get-tuple-element.310), kind=kOutput, calls=%fused_computation.197.clone.1 | convolution fusion | flops 12582912 | bytes 4259840 | tf_op jit(solution)/shard_map/while/body/eval_jaxpr/rhkv,rhk->rhv/dot_general | solution.py:129
  280.5 5.4 %fusion.68 = f32[8,8,1,128]{3,2,1,0:T(1,128)S(1)} fusion(f32[8,8,128,1]{2,3,1,0:T(1,128)S(1)} %bitcast.164, f32[8,8,128,128]{3,2,1,0:T(8,128)} %get-tuple-element.310), kind=kOutput, calls=%fused_computation.197.clone.1 | convolution fusion | flops 12582912 | bytes 4259840 | tf_op jit(solution)/shard_map/while/body/eval_jaxpr/rhkv,rhk->rhv/dot_general | solution.py:129
  295.6 5.4 %fusion.68 = f32[8,8,1,128]{3,2,1,0:T(1,128)S(1)} fusion(f32[8,8,128,1]{2,3,1,0:T(1,128)S(1)} %bitcast.164, f32[8,8,128,128]{3,2,1,0:T(8,128)} %get-tuple-element.310), kind=kOutput, calls=%fused_computation.197.clone.1 | convolution fusion | flops 12582912 | bytes 4259840 | tf_op jit(solution)/shard_map/while/body/eval_jaxpr/rhkv,rhk->rhv/dot_general | solution.py:129
  310.8 5.4 %fusion.68 = f32[8,8,1,128]{3,2,1,0:T(1,128)S(1)} fusion(f32[8,8,128,1]{2,3,1,0:T(1,128)S(1)} %bitcast.164, f32[8,8,128,128]{3,2,1,0:T(8,128)} %get-tuple-element.310), kind=kOutput, calls=%fused_computation.197.clone.1 | convolution fusion | flops 12582912 | bytes 4259840 | tf_op jit(solution)/shard_map/while/body/eval_jaxpr/rhkv,rhk->rhv/dot_general | solution.py:129
  332.9 4.6 %collective-permute-start.7 = (bf16[4,3,3,1024]{3,0,2,1:T(4,128)(2,1)S(1)}, bf16[4,3,3,1024]{3,0,2,1:T(4,128)(2,1)}, u32[]{:S(2)}, u32[]{:S(2)}) collective-permute-start(bf16[4,3,3,1024]{3,0,2,1:T(4,128)(2,1)S(1)} %fusion.20), channel_id=1, source_target_pairs={{0,2},{2,4},{4,6},{6,8},{8,10},{10,12},{12,14},{14,16},{16,18},{18... | collective-permute-start | bytes 221192 | tf_op jit(solution)/shard_map/ppermute | solution.py:14
  345.8 34.4 %collective-permute-done.7 = bf16[4,3,3,1024]{3,0,2,1:T(4,128)(2,1)} collective-permute-done((bf16[4,3,3,1024]{3,0,2,1:T(4,128)(2,1)S(1)}, bf16[4,3,3,1024]{3,0,2,1:T(4,128)(2,1)}, u32[]{:S(2)}, u32[]{:S(2)}) %collective-permute-start.7) | collective-permute-done | bytes 73760 | tf_op jit(solution)/shard_map/ppermute | solution.py:14
  (426 shorter events, 226.9 us)
Async XLA Ops:
  7.2 31.8 %copy-start = (bf16[2048,8]{0,1:T(8,128)(2,1)S(1)}, bf16[2048,8]{0,1:T(8,128)(2,1)}, u32[]{:S(2)}) copy-start(bf16[2048,8]{0,1:T(8,128)(2,1)} %param.27) | copy-start | bytes 98308
  7.2 13.5 %copy-start.6 = (bf16[8,8,128,128]{3,2,1,0:T(8,128)(2,1)S(1)}, bf16[8,8,128,128]{3,2,1,0:T(8,128)(2,1)}, u32[]{:S(2)}) copy-start(bf16[8,8,128,128]{3,2,1,0:T(8,128)(2,1)} %param.31) | copy-start | bytes 6291460
  7.2 387.3 %reduce-scatter.2.cloned.1.call-start = ((), (), s32[]{:S(2)}) async-start(), calls=%async_computation.1 | async-start | bytes 786432 | tf_op jit(solution)/shard_map/reduce_scatter | solution.py:143
  11.3 34.8 %collective-permute-start.3 = (bf16[4,3,3,1024]{3,0,2,1:T(4,128)(2,1)S(1)}, bf16[4,3,3,1024]{3,0,2,1:T(4,128)(2,1)S(1)}, u32[]{:S(2)}, u32[]{:S(2)}) collective-permute-start(bf16[4,3,3,1024]{3,0,2,1:T(4,128)(2,1)S(1)} %select_select_fusion.5), channel_id=1, source_target_pairs={{0,30},{2,0},{4,2},{6,4},{8,6},{10,8},{12,10},{14,12},{16,14},{18,... | collective-permute-start | bytes 221192 | tf_op jit(solution)/shard_map/ppermute | solution.py:14
  20.6 25.5 %collective-permute-start.2 = (bf16[4,3,3,1024]{3,0,2,1:T(4,128)(2,1)S(1)}, bf16[4,3,3,1024]{3,0,2,1:T(4,128)(2,1)}, u32[]{:S(2)}, u32[]{:S(2)}) collective-permute-start(bf16[4,3,3,1024]{3,0,2,1:T(4,128)(2,1)S(1)} %select_select_fusion.6), channel_id=1, source_target_pairs={{0,2},{2,4},{4,6},{6,8},{8,10},{10,12},{12,14},{14,16},{16,18},{18... | collective-permute-start | bytes 221192 | tf_op jit(solution)/shard_map/ppermute | solution.py:14
  22.6 45.2 %collective-permute-start = (bf16[4,8,128,128]{3,2,1,0:T(8,128)(2,1)}, bf16[4,8,128,128]{3,2,1,0:T(8,128)(2,1)}, u32[]{:S(2)}, u32[]{:S(2)}) collective-permute-start(bf16[4,8,128,128]{3,2,1,0:T(8,128)(2,1)} %select_select_fusion.4), channel_id=1, source_target_pairs={{0,2},{2,4},{4,6},{6,8},{8,10},{10,12},{12,14},{14,16},{16,18},{18... | collective-permute-start | bytes 3145736 | tf_op jit(solution)/shard_map/ppermute | solution.py:14
  23.4 12.8 %copy-start.32 = (bf16[2048]{0:T(1024)(128)(2,1)S(1)}, bf16[2048]{0:T(1024)(128)(2,1)}, u32[]{:S(2)}) copy-start(bf16[2048]{0:T(1024)(128)(2,1)} %param.25) | copy-start | bytes 12292
  23.5 12.8 %copy-start.10 = (bf16[4,3,1024]{2,0,1:T(4,128)(2,1)S(1)}, bf16[4,3,1024]{2,0,1:T(4,128)(2,1)}, u32[]{:S(2)}) copy-start(bf16[4,3,1024]{2,0,1:T(4,128)(2,1)} %param.28) | copy-start | bytes 73732
  23.5 12.8 %copy-start.8 = (bf16[8,16,1024]{2,1,0:T(8,128)(2,1)S(1)}, bf16[8,16,1024]{2,1,0:T(8,128)(2,1)}, u32[]{:S(2)}) copy-start(bf16[8,16,1024]{2,1,0:T(8,128)(2,1)} %param.24) | copy-start | bytes 786436
  24.7 43.2 %collective-permute-start.1 = (bf16[4,8,128,128]{3,2,1,0:T(8,128)(2,1)}, bf16[4,8,128,128]{3,2,1,0:T(8,128)(2,1)}, u32[]{:S(2)}, u32[]{:S(2)}) collective-permute-start(bf16[4,8,128,128]{3,2,1,0:T(8,128)(2,1)} %select_select_fusion.3), channel_id=1, source_target_pairs={{0,30},{2,0},{4,2},{6,4},{8,6},{10,8},{12,10},{14,12},{16,14},{18,... | collective-permute-start | bytes 3145736 | tf_op jit(solution)/shard_map/ppermute | solution.py:14
  33.8 14.3 %copy-start.33 = (pred[8]{0:T(512)(128)(4,1)}, pred[8]{0:T(512)(128)(4,1)S(1)}, u32[]{:S(2)}) copy-start(pred[8]{0:T(512)(128)(4,1)S(1)} %compare_and_fusion.7) | copy-start | bytes 28
  55.8 12.0 %copy-start.7 = (bf16[8,8,128,128]{3,2,1,0:T(8,128)(2,1)S(1)}, bf16[8,8,128,128]{3,2,1,0:T(8,128)(2,1)}, u32[]{:S(2)}) copy-start(bf16[8,8,128,128]{3,2,1,0:T(8,128)(2,1)} %param.31) | copy-start | bytes 6291460
  329.1 11.0 %copy-start.26 = (pred[4]{0:T(512)(128)(4,1)S(1)}, pred[4]{0:T(512)(128)(4,1)}, u32[]{:S(2)}) copy-start(pred[4]{0:T(512)(128)(4,1)} %copy-done.25) | copy-start | bytes 16
  329.1 11.0 %copy-start.29 = (pred[4]{0:T(512)(128)(4,1)S(1)}, pred[4]{0:T(512)(128)(4,1)}, u32[]{:S(2)}) copy-start(pred[4]{0:T(512)(128)(4,1)} %get-tuple-element.217) | copy-start | bytes 16
  330.3 62.0 %collective-permute-start.5 = (bf16[4,8,128,128]{3,2,1,0:T(8,128)(2,1)}, bf16[4,8,128,128]{3,2,1,0:T(8,128)(2,1)S(1)}, u32[]{:S(2)}, u32[]{:S(2)}) collective-permute-start(bf16[4,8,128,128]{3,2,1,0:T(8,128)(2,1)} %select_select_fusion.1), channel_id=1, source_target_pairs={{0,2},{2,4},{4,6},{6,8},{8,10},{10,12},{12,14},{14,16},{16,18},{18... | collective-permute-start | bytes 3145736 | tf_op jit(solution)/shard_map/ppermute | solution.py:14
  332.9 47.2 %collective-permute-start.7 = (bf16[4,3,3,1024]{3,0,2,1:T(4,128)(2,1)S(1)}, bf16[4,3,3,1024]{3,0,2,1:T(4,128)(2,1)}, u32[]{:S(2)}, u32[]{:S(2)}) collective-permute-start(bf16[4,3,3,1024]{3,0,2,1:T(4,128)(2,1)S(1)} %fusion.20), channel_id=1, source_target_pairs={{0,2},{2,4},{4,6},{6,8},{8,10},{10,12},{12,14},{14,16},{16,18},{18... | collective-permute-start | bytes 221192 | tf_op jit(solution)/shard_map/ppermute | solution.py:14
  340.1 47.9 %copy-start.11 = (pred[8]{0:T(512)(128)(4,1)S(1)}, pred[8]{0:T(512)(128)(4,1)}, u32[]{:S(2)}) copy-start(pred[8]{0:T(512)(128)(4,1)} %get-tuple-element.210) | copy-start | bytes 28
  340.1 47.9 %copy-start.13 = (pred[8]{0:T(512)(128)(4,1)S(1)}, pred[8]{0:T(512)(128)(4,1)}, u32[]{:S(2)}) copy-start(pred[8]{0:T(512)(128)(4,1)} %get-tuple-element.213) | copy-start | bytes 28
  340.1 47.9 %copy-start.16 = (pred[8]{0:T(512)(128)(4,1)S(1)}, pred[8]{0:T(512)(128)(4,1)}, u32[]{:S(2)}) copy-start(pred[8]{0:T(512)(128)(4,1)} %copy-done.15) | copy-start | bytes 28
  340.1 47.9 %copy-start.19 = (pred[8]{0:T(512)(128)(4,1)S(1)}, pred[8]{0:T(512)(128)(4,1)}, u32[]{:S(2)}) copy-start(pred[8]{0:T(512)(128)(4,1)} %copy-done.18) | copy-start | bytes 28
  340.1 47.9 %copy-start.21 = (pred[8]{0:T(512)(128)(4,1)S(1)}, pred[8]{0:T(512)(128)(4,1)}, u32[]{:S(2)}) copy-start(pred[8]{0:T(512)(128)(4,1)} %get-tuple-element.177) | copy-start | bytes 28
  340.1 47.9 %copy-start.23 = (pred[8]{0:T(512)(128)(4,1)S(1)}, pred[8]{0:T(512)(128)(4,1)}, u32[]{:S(2)}) copy-start(pred[8]{0:T(512)(128)(4,1)} %get-tuple-element.226) | copy-start | bytes 28
  342.5 53.9 %collective-permute-start.4 = (bf16[4,8,128,128]{3,2,1,0:T(8,128)(2,1)}, bf16[4,8,128,128]{3,2,1,0:T(8,128)(2,1)}, u32[]{:S(2)}, u32[]{:S(2)}) collective-permute-start(bf16[4,8,128,128]{3,2,1,0:T(8,128)(2,1)} %select_select_fusion.2), channel_id=1, source_target_pairs={{0,30},{2,0},{4,2},{6,4},{8,6},{10,8},{12,10},{14,12},{16,14},{18,... | collective-permute-start | bytes 3145736 | tf_op jit(solution)/shard_map/ppermute | solution.py:14
  344.4 41.3 %collective-permute-start.6 = (bf16[4,3,3,1024]{3,0,2,1:T(4,128)(2,1)}, bf16[4,3,3,1024]{3,0,2,1:T(4,128)(2,1)}, u32[]{:S(2)}, u32[]{:S(2)}) collective-permute-start(bf16[4,3,3,1024]{3,0,2,1:T(4,128)(2,1)} %fusion.21), channel_id=1, source_target_pairs={{0,30},{2,0},{4,2},{6,4},{8,6},{10,8},{12,10},{14,12},{16,14},{18,... | collective-permute-start | bytes 221192 | tf_op jit(solution)/shard_map/ppermute | solution.py:14
  (56 other events, 273.2 us)
Sparse Core Ops, SparseCore 0:
  328.5 11.0 reduce-scatter.1
where the time goes:
time: 414 us; the launch traced here: 411 us
  matrix products  156 us (38%)
  other arithmetic  102 us (25%)
  local copies, waits for them, and re-layouts  57.5 us (14%)
  waiting for transfers between devices  48.3 us (12%)
  starting transfers between devices  20.9 us (5%)
  between operations  14.9 us (4%)
  loops' own time  9.89 us (2%)
    dot_general x16, matrix products, advance(): jnp.einsum('rhkv,rhk->rhv', state, key_t, precision=lax.Precision.HIGHEST)  86.8 us
    dot_general x16, matrix products, advance(): jnp.einsum('rhkv,rhk->rhv', state, query, precision=lax.Precision.HIGHEST)  58.4 us
    ppermute x8, waiting for transfers between devices, passed_along(): lax.ppermute(array, axis, [(i, (i + by) % count) for i in range(count)])  48.3 us
    select_n x16, other arithmetic, advance(): jnp.where((kept == index + 1)[:, None, None, None], state, snapshot)  41 us
    ppermute x8, starting transfers between devices, passed_along(): lax.ppermute(array, axis, [(i, (i + by) % count) for i in range(count)])  20.9 us
    dynamic_slice x32, local copies, waits for them, and re-layouts, mix_layer(): lax.scan(advance, (start, start), steps_in)  19.6 us
    mul x16, other arithmetic, advance(): rate[..., None] * key_t  13.4 us
    sub x16, other arithmetic, advance(): value - recalled  12.4 us
  transfers between devices with their start and end apart: 9, of which 3 were waited for; matrix products, arithmetic and copies ran while one was open for 13% of the time, Pallas kernels for 0%

commit v1 on v0

v1 whole, which is shorter than its diff:
```python
import functools

import jax
import jax.numpy as jnp
from jax import lax
from jax.experimental import pallas as pl
from jax.experimental.pallas import tpu as pltpu
from jax.sharding import PartitionSpec as P

DK = 128
CONV = 4
MOVE = 4
HIST = CONV - 1
EXT0 = 8 - HIST
F32 = jnp.float32
BF16 = jnp.bfloat16
MESH = pl.DeviceIdType.MESH


def split(wide):
    high = wide.astype(BF16)
    return high, (wide - high.astype(F32)).astype(BF16)


def unit(values):
    return values * lax.rsqrt(jnp.sum(values * values, axis=-1, keepdims=True) + 1e-06)


def matches(po_ref, device, home, reqs):
    found = []
    count = jnp.int32(0)
    for j in range(reqs):
        request = po_ref[device * reqs + j]
        hit = (request >= home * reqs) & (request < home * reqs + reqs)
        found.append((request, hit, count))
        count = count + hit.astype(jnp.int32)
    return found


def pick_rank(found, rank, values):
    total = jnp.int32(0)
    for (_, hit, place), value in zip(found, values):
        total = total + jnp.where(hit & (place == rank), value, 0)
    return jnp.clip(total, 0, len(values) - 1)


def kernel(
    n_seq,
    n_tp,
    po_ref,
    len_ref,
    acc_ref,
    tok_ref,
    gain_ref,
    wb_ref,
    cw_ref,
    og_ref,
    conv_ref,
    wqkv_hbm,
    wout_hbm,
    state_hbm,
    mixed_ref,
    fconv_ref,
    pages_hbm,
    wq,
    wo,
    st,
    pool,
    send_l,
    send_r,
    xs,
    normed,
    ext,
    beta,
    on,
    kc,
    uc,
    part,
    part_in,
    done,
    back,
    back_l,
    back_r,
    w_sem,
    wo_sem,
    st_sem,
    out_sem,
    mig_send,
    mig_recv,
    tp_send,
    tp_recv,
    rs_send,
    rs_recv,
    ret_send,
    ret_recv,
):
    reqs, drafts, cols = tok_ref.shape
    rows = reqs * drafts
    heads = state_hbm.shape[1]
    hidden = heads * DK
    group = 2 if heads % 2 == 0 else 1
    width = group * DK
    tiles = heads // group
    me = lax.axis_index("seq")
    mt = lax.axis_index("tp")
    left = lax.rem(me + n_seq - 1, n_seq)
    right = lax.rem(me + 1, n_seq)

    def w_copy(i):
        at = pl.ds(pl.multiple_of(i * width, width), width)
        return pltpu.make_async_copy(wqkv_hbm.at[:, :, at], wq.at[:, :, at], w_sem.at[i])

    st_copy = pltpu.make_async_copy(state_hbm, st, st_sem)
    wo_copy = pltpu.make_async_copy(wout_hbm, wo, wo_sem)
    w_copy(0).start()
    st_copy.start()
    for i in range(1, tiles):
        w_copy(i).start()
    wo_copy.start()

    barrier = pltpu.get_barrier_semaphore()
    for other in (left, right):
        pl.semaphore_signal(barrier, inc=1, device_id={"seq": other}, device_id_type=MESH)
    for j in range(1, n_tp):
        pl.semaphore_signal(
            barrier, inc=1, device_id={"tp": lax.rem(mt + j, n_tp)}, device_id_type=MESH
        )

    own = matches(po_ref, me, me, reqs)
    from_l = matches(po_ref, me, left, reqs)
    from_r = matches(po_ref, me, right, reqs)
    at_l = matches(po_ref, left, me, reqs)
    at_r = matches(po_ref, right, me, reqs)
    base = me * reqs
    for k in range(MOVE):
        send_l[k] = tok_ref[pick_rank(at_l, k, [f[0] - base for f in at_l])]
        send_r[k] = tok_ref[pick_rank(at_r, k, [f[0] - base for f in at_r])]
    pl.semaphore_wait(barrier, 2 + n_tp - 1)

    def exchange(src_l, src_r, dst, send_sem, recv_sem):
        to_r = pltpu.make_async_remote_copy(
            src_ref=src_r,
            dst_ref=dst.at[pl.ds(reqs, MOVE)],
            send_sem=send_sem.at[0],
            recv_sem=recv_sem.at[0],
            device_id={"seq": right},
            device_id_type=MESH,
        )
        to_l = pltpu.make_async_remote_copy(
            src_ref=src_l,
            dst_ref=dst.at[pl.ds(reqs + MOVE, MOVE)],
            send_sem=send_sem.at[1],
            recv_sem=recv_sem.at[1],
            device_id={"seq": left},
            device_id_type=MESH,
        )
        to_r.start()
        to_l.start()
        return to_r, to_l

    moves = exchange(send_l, send_r, pool.at[mt], mig_send, mig_recv)

    def to_peers(src, dst, stage):
        copies = []
        for j in range(1, n_tp):
            copy = pltpu.make_async_remote_copy(
                src_ref=src,
                dst_ref=dst,
                send_sem=tp_send.at[stage, j],
                recv_sem=tp_recv.at[stage, j],
                device_id={"tp": lax.rem(mt + j, n_tp)},
                device_id_type=MESH,
            )
            copy.start()
            copies.append(copy)
        return copies

    gathers = to_peers(tok_ref, pool.at[mt, pl.ds(0, reqs)], 0)
    pool[mt, pl.ds(0, reqs)] = tok_ref[...]

    lengths = []
    keeps = []
    places = []
    for j in range(reqs):
        request, hit, _ = own[j]
        lengths.append(len_ref[request])
        keeps.append(jnp.minimum(acc_ref[request], lengths[j]))
        place = jnp.where(from_l[j][1], reqs + from_l[j][2], reqs + MOVE + from_r[j][2])
        place = jnp.where(hit, request - base, place)
        places.append(jnp.clip(place, 0, reqs + 2 * MOVE - 1))
    homes = []
    for i in range(reqs):
        place = jnp.int32(0)
        for j in range(reqs):
            place = jnp.where(own[j][0] == base + i, j, place)
            place = jnp.where(at_l[j][0] == base + i, reqs + at_l[j][2], place)
            place = jnp.where(at_r[j][0] == base + i, reqs + MOVE + at_r[j][2], place)
        homes.append(jnp.clip(place, 0, reqs + 2 * MOVE - 1))
    slots = list(range(reqs))
    back_to_l = [pick_rank(from_l, k, slots) for k in range(MOVE)]
    back_to_r = [pick_rank(from_r, k, slots) for k in range(MOVE)]
    req_of = lax.broadcasted_iota(jnp.int32, (reqs, drafts, 1), 0)
    step_of = lax.broadcasted_iota(jnp.int32, (reqs, drafts, 1), 1)
    live = jnp.zeros((reqs, drafts, 1), jnp.int32)
    kept = jnp.zeros((reqs, drafts, 1), jnp.int32)
    for j in range(reqs):
        live = jnp.where(req_of == j, lengths[j], live)
        kept = jnp.where(req_of == j, keeps[j], kept)
    live = (step_of < live).astype(F32)
    kept = (step_of < kept).astype(F32)
    for e in range(HIST):
        for c in range(3):
            ext[c, :, EXT0 + e, :] = conv_ref[e, c].astype(F32)

    for copy in moves:
        copy.wait()
    gathers += to_peers(
        pool.at[mt, pl.ds(reqs, 2 * MOVE)], pool.at[mt, pl.ds(reqs, 2 * MOVE)], 1
    )
    for copy in gathers:
        copy.wait()

    gain = gain_ref[...].astype(F32)
    for j in range(reqs):
        for c in range(n_tp):
            xs[j, :, pl.ds(c * cols, cols)] = pool[c, places[j]]
        wide = xs[j].astype(F32)
        scale = lax.rsqrt(jnp.mean(wide * wide, axis=-1, keepdims=True) + 1e-06)
        normed[pl.ds(j * drafts, drafts), :] = (wide * scale * gain).astype(BF16)
    rates = jax.nn.sigmoid(
        lax.dot_general(
            normed[...], wb_ref[...], (((1,), (1,)), ((), ())), preferred_element_type=F32
        )
    )
    beta[...] = rates * live.reshape(rows, 1)

    st_copy.wait()
    row_of = lax.broadcasted_iota(jnp.int32, (rows, rows), 0)
    col_of = lax.broadcasted_iota(jnp.int32, (rows, rows), 1)
    causal = (row_of // drafts == col_of // drafts) & (col_of <= row_of)
    half = drafts // 2
    t_half = lax.broadcasted_iota(jnp.int32, (1, half, 1), 1)
    head_of = lax.broadcasted_iota(jnp.int32, (rows, heads), 1)
    out_gain = og_ref[...].astype(F32)

    def tile(i, _):
        at = pl.ds(pl.multiple_of(i * width, width), width)
        w_copy(i).wait()
        acts = []
        for c in range(3):
            proj = jnp.dot(normed[...], wq[c, :, at], preferred_element_type=F32)
            ext[c, :, pl.ds(8, drafts), at] = (
                proj.astype(BF16).astype(F32).reshape(reqs, drafts, width)
            )
            taps = cw_ref[c, :, at].astype(F32)
            total = jnp.zeros((reqs, drafts, width), F32)
            for o in range(CONV):
                tap = taps[o : o + 1]
                total = total + ext[c, :, pl.ds(EXT0 + o, drafts), at] * tap
            acts.append(total * jax.nn.sigmoid(total))
        for g in range(group):
            h = i * group + g
            mine = slice(g * DK, (g + 1) * DK)
            q = unit(acts[0][:, :, mine]) * DK ** (-0.5)
            k = unit(acts[1][:, :, mine])
            v = acts[2][:, :, mine]
            rate = jnp.sum(jnp.where(head_of == h, beta[...], 0.0), axis=-1, keepdims=True)
            rate = rate.reshape(reqs, drafts, 1)
            kh, kl = split(k)
            qh = q.astype(BF16)
            stacked = jnp.concatenate([kh, kl, qh], axis=1)
            recalled = []
            seen = []
            for r in range(reqs):
                got = jnp.dot(stacked[r], st[r, h], preferred_element_type=F32)
                recalled.append(got[:drafts] + got[drafts : 2 * drafts])
                seen.append(got[2 * drafts :])
            u = rate * (v - jnp.stack(recalled))
            k0, k1 = k[:, :half], k[:, half:]
            rate0, rate1 = rate[:, :half], rate[:, half:]
            u0, u1 = u[:, :half], u[:, half:]
            for s in range(drafts - 1):
                if s < half:
                    key_s, u_s = k0[:, s : s + 1], u0[:, s : s + 1]
                else:
                    key_s, u_s = k1[:, s - half : s - half + 1], u1[:, s - half : s - half + 1]
                if s < half - 1:
                    near = jnp.sum(k0 * key_s, axis=-1, keepdims=True) * rate0
                    u0 = u0 - jnp.where(t_half > s, near, 0.0) * u_s
                near = jnp.sum(k1 * key_s, axis=-1, keepdims=True) * rate1
                if s >= half:
                    near = jnp.where(t_half + half > s, near, 0.0)
                u1 = u1 - near * u_s
            u = jnp.concatenate([u0, u1], axis=1)
            uh = u.astype(BF16)
            near = lax.dot_general(
                qh.reshape(rows, DK),
                kh.reshape(rows, DK),
                (((1,), (1,)), ((), ())),
                preferred_element_type=F32,
            )
            near = jnp.where(causal, near, 0.0).astype(BF16)
            o = jnp.stack(seen).reshape(rows, DK) + jnp.dot(
                near, uh.reshape(rows, DK), preferred_element_type=F32
            )
            scale = lax.rsqrt(jnp.mean(o * o, axis=-1, keepdims=True) + 1e-06)
            on[:, pl.ds(pl.multiple_of(h * DK, DK), DK)] = (o * scale * out_gain).astype(BF16)
            mh, ml = split(u * kept)
            kc[h] = jnp.concatenate([kh, kl, kh], axis=1)
            uc[h] = jnp.concatenate([mh, mh, ml], axis=1)
        return 0

    lax.fori_loop(0, tiles, tile, 0)

    wo_copy.wait()
    sums = []
    for j in list(range(1, n_tp)) + [0]:
        to = lax.rem(mt + j, n_tp)
        at = pl.ds(pl.multiple_of(to * cols, cols), cols)
        part[j] = jnp.dot(on[...], wo[:, at], preferred_element_type=F32).astype(BF16)
        if j:
            copy = pltpu.make_async_remote_copy(
                src_ref=part.at[j],
                dst_ref=part_in.at[j],
                send_sem=rs_send.at[j],
                recv_sem=rs_recv.at[j],
                device_id={"tp": to},
                device_id_type=MESH,
            )
            copy.start()
            sums.append(copy)
    mine = pl.ds(pl.multiple_of(mt * cols, cols), cols)
    total = part[0].astype(F32)
    for copy in sums:
        copy.wait()
    for j in range(1, n_tp):
        total = total + part_in[j].astype(F32)
    total = xs[:, :, mine].astype(F32) + total.reshape(reqs, drafts, cols)
    done[...] = jnp.where(live > 0, total, 0.0).astype(BF16)
    for k in range(MOVE):
        back_l[k] = done[back_to_l[k]]
        back_r[k] = done[back_to_r[k]]
    returns = exchange(back_l, back_r, back, ret_send, ret_recv)

    back[pl.ds(0, reqs)] = done[...]

    def page_copy(h):
        return pltpu.make_async_copy(st.at[:, h], pages_hbm.at[:, h], out_sem.at[h])

    def accept(h, _):
        for r in range(reqs):
            gained = lax.dot_general(
                kc[h, r], uc[h, r], (((0,), (0,)), ((), ())), preferred_element_type=F32
            )
            st[r, h] = (st[r, h].astype(F32) + gained).astype(BF16)
        page_copy(h).start()
        return 0

    lax.fori_loop(0, heads, accept, 0)
    line_of = lax.broadcasted_iota(jnp.int32, (reqs, 8 + drafts, 1), 1)
    req_line = lax.broadcasted_iota(jnp.int32, (reqs, 8 + drafts, 1), 0)
    first = jnp.zeros((reqs, 8 + drafts, 1), jnp.int32)
    for j in range(reqs):
        first = jnp.where(req_line == j, EXT0 + keeps[j], first)

    def edges(c, _):
        for e in range(HIST):
            chosen = jnp.where(line_of == first + e, ext[c], 0.0)
            fconv_ref[e, c] = jnp.sum(chosen, axis=1).astype(BF16)
        return 0

    lax.fori_loop(0, 3, edges, 0)

    for copy in returns:
        copy.wait()
    for i in range(reqs):
        mixed_ref[i] = back[homes[i]]

    def drain(h, _):
        page_copy(h).wait()
        return 0

    lax.fori_loop(0, heads, drain, 0)


def on_device(
    n_seq,
    n_tp,
    tokens,
    gain_in,
    w_qkv,
    w_beta,
    conv_weight,
    out_gain,
    w_out,
    state_pages,
    conv_pages,
    page_order,
    draft_lengths,
    accepted,
):
    reqs, drafts, cols = tokens.shape
    rows = reqs * drafts
    depth = w_qkv.shape[1]
    heads = state_pages.shape[1]
    hidden = heads * DK
    smem = pl.BlockSpec(memory_space=pltpu.SMEM)
    vmem = pl.BlockSpec(memory_space=pltpu.VMEM)
    hbm = pl.BlockSpec(memory_space=pl.ANY)
    dma = pltpu.SemaphoreType.DMA
    mixed, final_conv, pages = pl.pallas_call(
        functools.partial(kernel, n_seq, n_tp),
        out_shape=(
            jax.ShapeDtypeStruct(tokens.shape, BF16),
            jax.ShapeDtypeStruct((HIST, 3, reqs, hidden), BF16),
            jax.ShapeDtypeStruct(state_pages.shape, BF16),
        ),
        in_specs=[smem] * 3 + [vmem] * 6 + [hbm] * 3,
        out_specs=(vmem, vmem, hbm),
        scratch_shapes=[
            pltpu.VMEM(w_qkv.shape, BF16),
            pltpu.VMEM(w_out.shape, BF16),
            pltpu.VMEM(state_pages.shape, BF16),
            pltpu.VMEM((n_tp, reqs + 2 * MOVE, drafts, cols), BF16),
            pltpu.VMEM((MOVE, drafts, cols), BF16),
            pltpu.VMEM((MOVE, drafts, cols), BF16),
            pltpu.VMEM((reqs, drafts, depth), BF16),
            pltpu.VMEM((rows, depth), BF16),
            pltpu.VMEM((3, reqs, 8 + drafts, hidden), F32),
            pltpu.VMEM((rows, heads), F32),
            pltpu.VMEM((rows, hidden), BF16),
            pltpu.VMEM((heads, reqs, 3 * drafts, DK), BF16),
            pltpu.VMEM((heads, reqs, 3 * drafts, DK), BF16),
            pltpu.VMEM((n_tp, rows, cols), BF16),
            pltpu.VMEM((n_tp, rows, cols), BF16),
            pltpu.VMEM(tokens.shape, BF16),
            pltpu.VMEM((reqs + 2 * MOVE, drafts, cols), BF16),
            pltpu.VMEM((MOVE, drafts, cols), BF16),
            pltpu.VMEM((MOVE, drafts, cols), BF16),
            dma((heads,)),
            dma,
            dma,
            dma((heads,)),
            dma((2,)),
            dma((2,)),
            dma((2, n_tp)),
            dma((2, n_tp)),
            dma((n_tp,)),
            dma((n_tp,)),
            dma((2,)),
            dma((2,)),
        ],
        compiler_params=pltpu.CompilerParams(
            collective_id=0, has_side_effects=True, vmem_limit_bytes=52 * 1024 * 1024
        ),
    )(
        page_order,
        draft_lengths,
        accepted,
        tokens,
        gain_in.reshape(1, -1),
        w_beta.T,
        jnp.transpose(conv_weight, (1, 0, 2)),
        out_gain.reshape(1, -1),
        jnp.transpose(conv_pages, (1, 2, 0, 3)),
        w_qkv,
        w_out,
        state_pages,
    )
    return mixed, pages, jnp.transpose(final_conv, (2, 0, 1, 3))


def solution(mesh):
    return jax.shard_map(
        functools.partial(on_device, mesh.shape["seq"], mesh.shape["tp"]),
        mesh=mesh,
        in_specs=(
            P("seq", None, "tp"),
            P(),
            P(None, None, "tp"),
            P(None, "tp"),
            P(None, None, "tp"),
            P(),
            P("tp", None),
            P("seq", "tp", None, None),
            P("seq", None, None, "tp"),
            P(),
            P(),
            P(),
        ),
        out_specs=(P("seq", None, "tp"), P("seq", "tp", None, None), P("seq", None, None, "tp")),
        check_vma=False,
    )
```

time: 414 us -> 46.8 us (0.11)
  matrix products: 156 us -> 0 us
  other arithmetic: 102 us -> 0 us
  waiting for transfers between devices: 48.3 us -> 0 us
  local copies, waits for them, and re-layouts: 57.5 us -> 11.2 us
  Pallas kernels: 0 us -> 34.6 us
  starting transfers between devices: 20.9 us -> 0 us
  between operations: 14.9 us -> 0.65 us
  loops' own time: 9.89 us -> 0 us
    dot_general x35 -> x0, matrix products: 156 us -> none  [the longest x16 86.8 us: advance(): jnp.einsum('rhkv,rhk->rhv', state, key_t, precision=lax.Precision.HIGHEST)]
    select_n x36 -> x0, other arithmetic: 54.7 us -> none  [the longest x16 41 us: advance(): jnp.where((kept == index + 1)[:, None, None, None], state, snapshot)]
    ppermute x8 -> x0, waiting for transfers between devices: 48.3 us -> none  [passed_along(): lax.ppermute(array, axis, [(i, (i + by) % count) for i in range(count)])]
    pallas_call x0 -> x1, Pallas kernels: none -> 34.6 us  [on_device(): pl.pallas_call(functools.partial(kernel, n_seq, n_tp), out_shape=(jax.Sha...]
    gather x20 -> x0, local copies, waits for them, and re-layouts: 28.8 us -> none  [the longest x8 9.04 us: select_rows(): rows = jnp.take(values, positions, axis=0)]
    ppermute x8 -> x0, starting transfers between devices: 20.9 us -> none  [passed_along(): lax.ppermute(array, axis, [(i, (i + by) % count) for i in range(count)])]
    dynamic_slice x32 -> x0, local copies, waits for them, and re-layouts: 19.6 us -> none  [mix_layer(): lax.scan(advance, (start, start), steps_in)]
    mul x17 -> x0, other arithmetic: 14.7 us -> none  [the longest x16 13.4 us: advance(): rate[..., None] * key_t]
  transfers between devices with their start and end apart: 9 -> 0, of which waited for: 3 -> 0; matrix products, arithmetic and copies ran while one was open for 13% -> 0% of each run, Pallas kernels for 0% -> 0%
where the time goes in v1:
time: 46.8 us; the launch traced here: 46.4 us
  Pallas kernels  34.6 us (74%)
  local copies, waits for them, and re-layouts  11.2 us (24%)
  between operations  0.65 us (1%)
    pallas_call x1, Pallas kernels, on_device(): pl.pallas_call(functools.partial(kernel, n_seq, n_tp), out_shape=(jax.Sha...  34.6 us
    unnamed x19, local copies, waits for them, and re-layouts  10.5 us

profile of v1, /device:TPU:0, one launch (start us, length us, event | category | flops | bytes accessed | tf_op | source)
XLA Modules:
  0.0 46.4 jit_solution(2517940640861282319)
XLA Ops:
  0.6 0.7 %reshape.12.gain_ref = bf16[1,2048]{1,0:T(2,128)(2,1)S(1)} reshape(bf16[2048]{0:T(1024)(128)(2,1)} %param.13) | data formatting | bytes 8192 | tf_op jit(solution)/shard_map/reshape | solution.py:461
  1.3 0.0 copy-start
  1.3 0.9 %copy-done = bf16[8,16,1024]{2,1,0:T(8,128)(2,1)S(1)} copy-done((bf16[8,16,1024]{2,1,0:T(8,128)(2,1)S(1)}, bf16[8,16,1024]{2,1,0:T(8,128)(2,1)}, u32[]{:S(2)}) %copy-start) | copy-done | bytes 262168
  2.3 0.0 copy-start.1
  2.3 0.9 %copy-done.1 = bf16[8,3,3,1024]{3,0,2,1:T(8,128)(2,1)S(1)} copy-done((bf16[8,3,3,1024]{3,0,2,1:T(8,128)(2,1)S(1)}, bf16[8,3,3,1024]{3,0,2,1:T(8,128)(2,1)}, u32[]{:S(2)}) %copy-start.1) | copy-done | bytes 147480
  3.2 0.0 copy-start.2
  3.2 0.8 %copy-done.2 = bf16[2048,8]{0,1:T(8,128)(2,1)S(1)} copy-done((bf16[2048,8]{0,1:T(8,128)(2,1)S(1)}, bf16[2048,8]{0,1:T(8,128)(2,1)}, u32[]{:S(2)}) %copy-start.2) | copy-done | bytes 32792
  3.9 0.0 copy-start.3
  3.9 0.7 %copy-done.3 = bf16[4,3,1024]{2,0,1:T(4,128)(2,1)S(1)} copy-done((bf16[4,3,1024]{2,0,1:T(4,128)(2,1)S(1)}, bf16[4,3,1024]{2,0,1:T(4,128)(2,1)}, u32[]{:S(2)}) %copy-start.3) | copy-done | bytes 24600
  4.7 0.0 copy-start.4
  4.7 0.7 %copy-done.4 = s32[128]{0:T(128)S(1)} copy-done((s32[128]{0:T(128)S(1)}, s32[128]{0:T(128)}, u32[]{:S(2)}) %copy-start.4) | copy-done | bytes 536
  5.3 0.0 copy-start.5
  5.3 0.7 %copy-done.5 = s32[128]{0:T(128)S(1)} copy-done((s32[128]{0:T(128)S(1)}, s32[128]{0:T(128)}, u32[]{:S(2)}) %copy-start.5) | copy-done | bytes 536
  6.0 0.0 copy-start.6
  6.0 0.7 %copy-done.6 = s32[128]{0:T(128)S(1)} copy-done((s32[128]{0:T(128)S(1)}, s32[128]{0:T(128)}, u32[]{:S(2)}) %copy-start.6) | copy-done | bytes 536
  6.6 0.0 copy-start.7
  6.7 0.7 %copy-done.7 = bf16[128]{0:T(256)(128)(2,1)S(1)} copy-done((bf16[128]{0:T(256)(128)(2,1)S(1)}, bf16[128]{0:T(256)(128)(2,1)}, u32[]{:S(2)}) %copy-start.7) | copy-done | bytes 280
  7.3 34.6 %shard_map.139 = (bf16[8,16,1024]{2,1,0:T(8,128)(2,1)S(1)}, bf16[3,3,8,1024]{3,2,1,0:T(8,128)(2,1)S(1)}, bf16[8,8,128,128]{3,2,1,0:T(8,128)(2,1)}) custom-call(s32[128]{0:T(128)S(1)} %copy-done.4, s32[128]{0:T(128)S(1)} %copy-done.5, s32[128]{0:T(128)S(1)} %copy-done.6, bf16[8,16,1024]{2,1,0:T(8,128)(2,1)S(1)} %copy-done, ...), custom_call_target="tpu_custom_call" | custom-call | tf_op jit(solution)/shard_map/pallas_call | solution.py:411
  41.9 0.7 %copy.18 = bf16[8,16,1024]{2,1,0:T(8,128)(2,1)} copy(bf16[8,16,1024]{2,1,0:T(8,128)(2,1)S(1)} %get-tuple-element.12) | data formatting | bytes 524288
  42.6 3.2 %copy.19 = bf16[8,8,128,128]{3,2,1,0:T(8,128)(2,1)} copy(bf16[8,8,128,128]{3,2,1,0:T(8,128)(2,1)} %get-tuple-element.13) | data formatting | bytes 4194304
  45.7 0.7 %copy.20 = bf16[8,3,3,1024]{3,0,2,1:T(8,128)(2,1)} copy(bf16[8,3,3,1024]{3,0,2,1:T(8,128)(2,1)S(1)} %bitcast.5) | data formatting | bytes 294912
Async XLA Ops:
  1.3 0.9 %copy-start = (bf16[8,16,1024]{2,1,0:T(8,128)(2,1)S(1)}, bf16[8,16,1024]{2,1,0:T(8,128)(2,1)}, u32[]{:S(2)}) copy-start(bf16[8,16,1024]{2,1,0:T(8,128)(2,1)} %tok_ref.1) | copy-start | bytes 786436
  2.3 0.9 %copy-start.1 = (bf16[8,3,3,1024]{3,0,2,1:T(8,128)(2,1)S(1)}, bf16[8,3,3,1024]{3,0,2,1:T(8,128)(2,1)}, u32[]{:S(2)}) copy-start(bf16[8,3,3,1024]{3,0,2,1:T(8,128)(2,1)} %param.20) | copy-start | bytes 442372
  3.2 0.8 %copy-start.2 = (bf16[2048,8]{0,1:T(8,128)(2,1)S(1)}, bf16[2048,8]{0,1:T(8,128)(2,1)}, u32[]{:S(2)}) copy-start(bf16[2048,8]{0,1:T(8,128)(2,1)} %param.15) | copy-start | bytes 98308
  3.9 0.7 %copy-start.3 = (bf16[4,3,1024]{2,0,1:T(4,128)(2,1)S(1)}, bf16[4,3,1024]{2,0,1:T(4,128)(2,1)}, u32[]{:S(2)}) copy-start(bf16[4,3,1024]{2,0,1:T(4,128)(2,1)} %param.16) | copy-start | bytes 73732
  4.7 0.7 %copy-start.4 = (s32[128]{0:T(128)S(1)}, s32[128]{0:T(128)}, u32[]{:S(2)}) copy-start(s32[128]{0:T(128)} %po_ref.1) | copy-start | bytes 1540
  5.3 0.7 %copy-start.5 = (s32[128]{0:T(128)S(1)}, s32[128]{0:T(128)}, u32[]{:S(2)}) copy-start(s32[128]{0:T(128)} %len_ref.1) | copy-start | bytes 1540
  6.0 0.7 %copy-start.6 = (s32[128]{0:T(128)S(1)}, s32[128]{0:T(128)}, u32[]{:S(2)}) copy-start(s32[128]{0:T(128)} %acc_ref.1) | copy-start | bytes 1540
  6.6 0.7 %copy-start.7 = (bf16[128]{0:T(256)(128)(2,1)S(1)}, bf16[128]{0:T(256)(128)(2,1)}, u32[]{:S(2)}) copy-start(bf16[128]{0:T(256)(128)(2,1)} %param.17) | copy-start | bytes 772

commit v2 on v1

v2 whole, which is shorter than its diff:
```python
import functools

import jax
import jax.numpy as jnp
from jax import lax
from jax.experimental import pallas as pl
from jax.experimental.pallas import tpu as pltpu
from jax.sharding import PartitionSpec as P

DK = 128
CONV = 4
MOVE = 4
HIST = CONV - 1
EXT0 = 8 - HIST
F32 = jnp.float32
BF16 = jnp.bfloat16
MESH = pl.DeviceIdType.MESH


def split(wide):
    high = wide.astype(BF16)
    return high, (wide - high.astype(F32)).astype(BF16)


def unit(values):
    return values * lax.rsqrt(jnp.sum(values * values, axis=-1, keepdims=True) + 1e-06)


def matches(po_ref, device, home, reqs):
    found = []
    count = jnp.int32(0)
    for j in range(reqs):
        request = po_ref[device * reqs + j]
        hit = (request >= home * reqs) & (request < home * reqs + reqs)
        found.append((request, hit, count))
        count = count + hit.astype(jnp.int32)
    return found


def pick_rank(found, rank, values):
    total = jnp.int32(0)
    for (_, hit, place), value in zip(found, values):
        total = total + jnp.where(hit & (place == rank), value, 0)
    return jnp.clip(total, 0, len(values) - 1)


def kernel(
    n_seq,
    n_tp,
    po_hbm,
    len_hbm,
    acc_hbm,
    tok_hbm,
    gain_hbm,
    wb_hbm,
    cw_hbm,
    og_hbm,
    conv_hbm,
    wqkv_hbm,
    wout_hbm,
    state_hbm,
    mixed_ref,
    fconv_ref,
    pages_hbm,
    po_ref,
    len_ref,
    acc_ref,
    tok_ref,
    gain_ref,
    wb_ref,
    cw_ref,
    og_ref,
    conv_ref,
    wq,
    wo,
    st,
    pool,
    send_l,
    send_r,
    xs,
    normed,
    ext,
    queries,
    keys,
    values,
    beta,
    on,
    kc,
    uc,
    part,
    part_in,
    done,
    back,
    pages_ref,
    in_sem,
    out_sem,
    w_sem,
    wo_sem,
    st_sem,
    mig_send,
    mig_recv,
    tp_send,
    tp_recv,
    rs_send,
    rs_recv,
    ret_send,
    ret_recv,
):
    reqs, drafts, cols = tok_ref.shape
    rows = reqs * drafts
    heads = state_hbm.shape[1]
    hidden = heads * DK
    group = 2 if heads % 2 == 0 else 1
    width = group * DK
    tiles = heads // group
    me = lax.axis_index("seq")
    mt = lax.axis_index("tp")
    left = lax.rem(me + n_seq - 1, n_seq)
    right = lax.rem(me + 1, n_seq)

    def w_copy(i):
        at = pl.ds(pl.multiple_of(i * width, width), width)
        return pltpu.make_async_copy(wqkv_hbm.at[:, :, at], wq.at[:, :, at], w_sem.at[i])

    st_copy = pltpu.make_async_copy(state_hbm, st, st_sem)
    wo_copy = pltpu.make_async_copy(wout_hbm, wo, wo_sem)
    small = []
    pairs = (
        (po_hbm, po_ref),
        (len_hbm, len_ref),
        (acc_hbm, acc_ref),
        (tok_hbm, tok_ref),
        (conv_hbm, conv_ref),
        (gain_hbm, gain_ref),
        (wb_hbm, wb_ref),
        (cw_hbm, cw_ref),
        (og_hbm, og_ref),
    )
    for i, (src, dst) in enumerate(pairs):
        small.append(pltpu.make_async_copy(src, dst, in_sem.at[i]))
        small[i].start()
    w_copy(0).start()
    st_copy.start()
    for i in range(1, tiles):
        w_copy(i).start()
    wo_copy.start()

    barrier = pltpu.get_barrier_semaphore()
    for other in (left, right):
        pl.semaphore_signal(barrier, inc=1, device_id={"seq": other}, device_id_type=MESH)
    for j in range(1, n_tp):
        pl.semaphore_signal(
            barrier, inc=1, device_id={"tp": lax.rem(mt + j, n_tp)}, device_id_type=MESH
        )

    for copy in small[:4]:
        copy.wait()
    own = matches(po_ref, me, me, reqs)
    from_l = matches(po_ref, me, left, reqs)
    from_r = matches(po_ref, me, right, reqs)
    at_l = matches(po_ref, left, me, reqs)
    at_r = matches(po_ref, right, me, reqs)
    base = me * reqs
    for k in range(MOVE):
        send_l[k] = tok_ref[pick_rank(at_l, k, [f[0] - base for f in at_l])]
        send_r[k] = tok_ref[pick_rank(at_r, k, [f[0] - base for f in at_r])]
    pl.semaphore_wait(barrier, 2 + n_tp - 1)

    def to_right(src, dst, send_sem, recv_sem):
        copy = pltpu.make_async_remote_copy(
            src_ref=src,
            dst_ref=dst.at[pl.ds(reqs, MOVE)],
            send_sem=send_sem.at[0],
            recv_sem=recv_sem.at[0],
            device_id={"seq": right},
            device_id_type=MESH,
        )
        copy.start()
        return copy

    def to_left(src, dst, send_sem, recv_sem):
        copy = pltpu.make_async_remote_copy(
            src_ref=src,
            dst_ref=dst.at[pl.ds(reqs + MOVE, MOVE)],
            send_sem=send_sem.at[1],
            recv_sem=recv_sem.at[1],
            device_id={"seq": left},
            device_id_type=MESH,
        )
        copy.start()
        return copy

    moves = [
        to_right(send_r, pool.at[mt], mig_send, mig_recv),
        to_left(send_l, pool.at[mt], mig_send, mig_recv),
    ]

    def to_peers(src, dst, stage):
        copies = []
        for j in range(1, n_tp):
            copy = pltpu.make_async_remote_copy(
                src_ref=src,
                dst_ref=dst,
                send_sem=tp_send.at[stage, j],
                recv_sem=tp_recv.at[stage, j],
                device_id={"tp": lax.rem(mt + j, n_tp)},
                device_id_type=MESH,
            )
            copy.start()
            copies.append(copy)
        return copies

    gathers = to_peers(tok_ref, pool.at[mt, pl.ds(0, reqs)], 0)
    pool[mt, pl.ds(0, reqs)] = tok_ref[...]

    count_l = jnp.int32(0)
    count_r = jnp.int32(0)
    for j in range(reqs):
        count_l = count_l + from_l[j][1].astype(jnp.int32)
        count_r = count_r + from_r[j][1].astype(jnp.int32)
    spot = []
    places = []
    for j in range(reqs):
        rank = own[j][2]
        room = MOVE - count_l
        here = jnp.where(rank < room, count_l + rank, MOVE + count_r + rank - room)
        other = jnp.where(from_l[j][1], from_l[j][2], MOVE + from_r[j][2])
        spot.append(jnp.clip(jnp.where(own[j][1], here, other), 0, reqs - 1))
        place = jnp.where(from_l[j][1], reqs + from_l[j][2], reqs + MOVE + from_r[j][2])
        place = jnp.where(own[j][1], own[j][0] - base, place)
        places.append(jnp.clip(place, 0, reqs + 2 * MOVE - 1))
    slot_at = []
    place_at = []
    lengths = []
    keeps = []
    for p in range(reqs):
        slot = jnp.int32(0)
        place = jnp.int32(0)
        request = jnp.int32(0)
        for j in range(reqs):
            hit = spot[j] == p
            slot = jnp.where(hit, j, slot)
            place = jnp.where(hit, places[j], place)
            request = jnp.where(hit, own[j][0], request)
        slot_at.append(slot)
        place_at.append(place)
        lengths.append(len_ref[request])
        keeps.append(jnp.minimum(acc_ref[request], lengths[p]))
    homes = []
    for i in range(reqs):
        place = jnp.int32(0)
        for j in range(reqs):
            place = jnp.where(own[j][0] == base + i, spot[j], place)
            place = jnp.where(at_l[j][0] == base + i, reqs + at_l[j][2], place)
            place = jnp.where(at_r[j][0] == base + i, reqs + MOVE + at_r[j][2], place)
        homes.append(jnp.clip(place, 0, reqs + 2 * MOVE - 1))

    def spread(numbers, shape):
        index = lax.broadcasted_iota(jnp.int32, shape, 0)
        out = jnp.zeros(shape, jnp.int32)
        for p in range(reqs):
            out = jnp.where(index == p, numbers[p], out)
        return out

    step_of = lax.broadcasted_iota(jnp.int32, (reqs, drafts, 1), 1)
    live = (step_of < spread(lengths, (reqs, drafts, 1))).astype(F32)
    kept = (step_of < spread(keeps, (reqs, drafts, 1))).astype(F32)
    lane_of = lax.broadcasted_iota(jnp.int32, (reqs, reqs), 1)
    to_spot = (lane_of == spread(slot_at, (reqs, reqs))).astype(F32).astype(BF16)
    to_slot = (lane_of == spread(spot, (reqs, reqs))).astype(F32).astype(BF16)
    for copy in small[4:]:
        copy.wait()
    for e in range(HIST):
        for c in range(3):
            ext[c, :, EXT0 + e, :] = jnp.dot(
                to_spot, conv_ref[e, c], preferred_element_type=F32
            )

    for copy in moves:
        copy.wait()
    gathers += to_peers(
        pool.at[mt, pl.ds(reqs, 2 * MOVE)], pool.at[mt, pl.ds(reqs, 2 * MOVE)], 1
    )
    for copy in gathers:
        copy.wait()

    gain = gain_ref[...].astype(F32).reshape(1, -1)
    for j in range(reqs):
        for c in range(n_tp):
            xs[j, :, pl.ds(c * cols, cols)] = pool[c, place_at[j]]
        wide = xs[j].astype(F32)
        scale = lax.rsqrt(jnp.mean(wide * wide, axis=-1, keepdims=True) + 1e-06)
        normed[pl.ds(j * drafts, drafts), :] = (wide * scale * gain).astype(BF16)
    rates = jax.nn.sigmoid(
        lax.dot_general(
            normed[...], wb_ref[...], (((1,), (1,)), ((), ())), preferred_element_type=F32
        )
    )
    beta[...] = rates * live.reshape(rows, 1)

    many = group * MOVE
    block = many * drafts
    row_of = lax.broadcasted_iota(jnp.int32, (block, block), 0)
    col_of = lax.broadcasted_iota(jnp.int32, (block, block), 1)
    causal = (row_of // drafts == col_of // drafts) & (col_of <= row_of)
    half = drafts // 2
    t_half = lax.broadcasted_iota(jnp.int32, (1, half, 1), 1)
    head_of = lax.broadcasted_iota(jnp.int32, (MOVE * drafts, heads), 1)
    out_gain = og_ref[...].astype(F32)

    def tile(i, _):
        at = pl.ds(pl.multiple_of(i * width, width), width)
        w_copy(i).wait()
        acts = []
        for c in range(3):
            proj = jnp.dot(normed[...], wq[c, :, at], preferred_element_type=F32)
            ext[c, :, pl.ds(8, drafts), at] = (
                proj.astype(BF16).astype(F32).reshape(reqs, drafts, width)
            )
            taps = cw_ref[c, :, at].astype(F32)
            total = jnp.zeros((reqs, drafts, width), F32)
            for o in range(CONV):
                tap = taps[o : o + 1]
                total = total + ext[c, :, pl.ds(EXT0 + o, drafts), at] * tap
            acts.append(total * jax.nn.sigmoid(total))
        for g in range(group):
            h = i * group + g
            mine = slice(g * DK, (g + 1) * DK)
            queries[h] = (unit(acts[0][:, :, mine]) * DK ** (-0.5)).astype(BF16)
            keys[h] = unit(acts[1][:, :, mine])
            values[h] = acts[2][:, :, mine]
        return 0

    lax.fori_loop(0, tiles, tile, 0)
    st_copy.wait()

    def delta(side):
        mine = pl.ds(side * MOVE, MOVE)
        kept_here = kept[side * MOVE : (side + 1) * MOVE]

        def heads_of(i, _):
            at = pl.ds(i * group, group)
            q = queries[at, mine].reshape(many, drafts, DK)
            k = keys[at, mine].reshape(many, drafts, DK)
            v = values[at, mine].reshape(many, drafts, DK)
            rate = []
            for g in range(group):
                rates = beta[pl.ds(side * MOVE * drafts, MOVE * drafts), :]
                rate.append(
                    jnp.sum(
                        jnp.where(head_of == i * group + g, rates, 0.0), axis=-1, keepdims=True
                    ).reshape(MOVE, drafts, 1)
                )
            rate = jnp.concatenate(rate, axis=0)
            kh, kl = split(k)
            stacked = jnp.concatenate([kh, kl, q], axis=1)
            recalled = []
            seen = []
            for g in range(group):
                for r in range(MOVE):
                    state = st[slot_at[side * MOVE + r], i * group + g]
                    got = jnp.dot(stacked[g * MOVE + r], state, preferred_element_type=F32)
                    recalled.append(got[:drafts] + got[drafts : 2 * drafts])
                    seen.append(got[2 * drafts :])
            u = rate * (v - jnp.stack(recalled))
            k0, k1 = k[:, :half], k[:, half:]
            rate0, rate1 = rate[:, :half], rate[:, half:]
            u0, u1 = u[:, :half], u[:, half:]
            for s in range(drafts - 1):
                if s < half:
                    key_s, u_s = k0[:, s : s + 1], u0[:, s : s + 1]
                else:
                    key_s, u_s = k1[:, s - half : s - half + 1], u1[:, s - half : s - half + 1]
                if s < half - 1:
                    near = jnp.sum(k0 * key_s, axis=-1, keepdims=True) * rate0
                    u0 = u0 - jnp.where(t_half > s, near, 0.0) * u_s
                near = jnp.sum(k1 * key_s, axis=-1, keepdims=True) * rate1
                if s >= half:
                    near = jnp.where(t_half + half > s, near, 0.0)
                u1 = u1 - near * u_s
            u = jnp.concatenate([u0, u1], axis=1)
            near = lax.dot_general(
                q.reshape(block, DK),
                kh.reshape(block, DK),
                (((1,), (1,)), ((), ())),
                preferred_element_type=F32,
            )
            near = jnp.where(causal, near, 0.0).astype(BF16)
            o = jnp.stack(seen).reshape(block, DK) + jnp.dot(
                near, u.astype(BF16).reshape(block, DK), preferred_element_type=F32
            )
            scale = lax.rsqrt(jnp.mean(o * o, axis=-1, keepdims=True) + 1e-06)
            o = (o * scale * out_gain).astype(BF16)
            rows_here = MOVE * drafts
            for g in range(group):
                columns = pl.ds(pl.multiple_of((i * group + g) * DK, DK), DK)
                on[pl.ds(side * rows_here, rows_here), columns] = o[
                    g * rows_here : (g + 1) * rows_here
                ]
            u = u.reshape(group, MOVE, drafts, DK) * kept_here[None]
            mh, ml = split(u.reshape(many, drafts, DK))
            shape = (group, MOVE, 3 * drafts, DK)
            kc[at, mine] = jnp.concatenate([kh, kl, kh], axis=1).reshape(shape)
            uc[at, mine] = jnp.concatenate([mh, mh, ml], axis=1).reshape(shape)
            return 0

        return heads_of

    def project(side):
        sums = []
        lines = pl.ds(side * MOVE * drafts, MOVE * drafts)
        for j in list(range(1, n_tp)) + [0]:
            to = lax.rem(mt + j, n_tp)
            at = pl.ds(pl.multiple_of(to * cols, cols), cols)
            part[side, j] = jnp.dot(
                on[lines, :], wo[:, at], preferred_element_type=F32
            ).astype(BF16)
            if j:
                copy = pltpu.make_async_remote_copy(
                    src_ref=part.at[side, j],
                    dst_ref=part_in.at[side, j],
                    send_sem=rs_send.at[side, j],
                    recv_sem=rs_recv.at[side, j],
                    device_id={"tp": to},
                    device_id_type=MESH,
                )
                copy.start()
                sums.append(copy)
        return sums

    def finish(side, sums):
        for copy in sums:
            copy.wait()
        total = part[side, 0].astype(F32)
        for j in range(1, n_tp):
            total = total + part_in[side, j].astype(F32)
        mine = pl.ds(side * MOVE, MOVE)
        columns = pl.ds(pl.multiple_of(mt * cols, cols), cols)
        total = xs[mine, :, columns].astype(F32) + total.reshape(MOVE, drafts, cols)
        live_here = live[side * MOVE : (side + 1) * MOVE]
        rows_done = jnp.where(live_here > 0, total, 0.0).astype(BF16)
        done[mine] = rows_done
        back[mine] = rows_done

    lax.fori_loop(0, tiles, delta(0), 0)
    wo_copy.wait()
    sums = project(0)
    second = delta(1)
    lax.fori_loop(0, 1, second, 0)
    finish(0, sums)
    returns = [to_left(done.at[pl.ds(0, MOVE)], back, ret_send, ret_recv)]
    lax.fori_loop(1, tiles, second, 0)
    sums = project(1)

    line_of = lax.broadcasted_iota(jnp.int32, (reqs, 8 + drafts, 1), 1)
    first = EXT0 + spread(keeps, (reqs, 8 + drafts, 1))

    def edges(c, _):
        for e in range(HIST):
            chosen = jnp.sum(jnp.where(line_of == first + e, ext[c], 0.0), axis=1)
            fconv_ref[e, c] = jnp.dot(
                to_slot, chosen.astype(BF16), preferred_element_type=F32
            ).astype(BF16)
        return 0

    lax.fori_loop(0, 3, edges, 0)
    finish(1, sums)
    returns.append(to_right(done.at[pl.ds(MOVE, MOVE)], back, ret_send, ret_recv))

    def page_copy(h):
        return pltpu.make_async_copy(pages_ref.at[:, h], pages_hbm.at[:, h], out_sem.at[h])

    def accept(h, _):
        for j in range(reqs):
            gained = lax.dot_general(
                kc[h, spot[j]], uc[h, spot[j]], (((0,), (0,)), ((), ())), preferred_element_type=F32
            )
            pages_ref[j, h] = (st[j, h].astype(F32) + gained).astype(BF16)
        page_copy(h).start()
        return 0

    def drain(h, _):
        page_copy(h).wait()
        return 0

    lax.fori_loop(0, heads, accept, 0)
    for copy in returns:
        copy.wait()
    for i in range(reqs):
        mixed_ref[i] = back[homes[i]]
    lax.fori_loop(0, heads, drain, 0)


def hand_out(mixed_in, fconv_in, pages_in, mixed_out, fconv_out, pages_out, sem):
    reqs = pages_in.shape[0]
    copies = [
        pltpu.make_async_copy(mixed_in, mixed_out, sem.at[reqs]),
        pltpu.make_async_copy(fconv_in, fconv_out, sem.at[reqs + 1]),
    ]
    for j in range(reqs):
        copies.append(pltpu.make_async_copy(pages_in.at[j], pages_out.at[j], sem.at[j]))
    for copy in copies:
        copy.start()
    for copy in copies:
        copy.wait()


def on_device(
    n_seq,
    n_tp,
    tokens,
    gain_in,
    w_qkv,
    w_beta,
    conv_weight,
    out_gain,
    w_out,
    state_pages,
    conv_pages,
    page_order,
    draft_lengths,
    accepted,
):
    reqs, drafts, cols = tokens.shape
    rows = reqs * drafts
    depth = w_qkv.shape[1]
    heads = state_pages.shape[1]
    hidden = heads * DK
    vmem = pl.BlockSpec(memory_space=pltpu.VMEM)
    hbm = pl.BlockSpec(memory_space=pltpu.HBM)
    dma = pltpu.SemaphoreType.DMA
    results = pl.pallas_call(
        functools.partial(kernel, n_seq, n_tp),
        out_shape=(
            jax.ShapeDtypeStruct(tokens.shape, BF16),
            jax.ShapeDtypeStruct((HIST, 3, reqs, hidden), BF16),
            jax.ShapeDtypeStruct(state_pages.shape, BF16),
        ),
        in_specs=[hbm] * 12,
        out_specs=(vmem, vmem, hbm),
        scratch_shapes=[
            pltpu.SMEM(page_order.shape, jnp.int32),
            pltpu.SMEM(draft_lengths.shape, jnp.int32),
            pltpu.SMEM(accepted.shape, jnp.int32),
            pltpu.VMEM(tokens.shape, BF16),
            pltpu.VMEM(gain_in.shape, BF16),
            pltpu.VMEM((heads, depth), BF16),
            pltpu.VMEM((3, CONV, hidden), BF16),
            pltpu.VMEM((1, DK), BF16),
            pltpu.VMEM((HIST, 3, reqs, hidden), BF16),
            pltpu.VMEM(w_qkv.shape, BF16),
            pltpu.VMEM(w_out.shape, BF16),
            pltpu.VMEM(state_pages.shape, BF16),
            pltpu.VMEM((n_tp, reqs + 2 * MOVE, drafts, cols), BF16),
            pltpu.VMEM((MOVE, drafts, cols), BF16),
            pltpu.VMEM((MOVE, drafts, cols), BF16),
            pltpu.VMEM((reqs, drafts, depth), BF16),
            pltpu.VMEM((rows, depth), BF16),
            pltpu.VMEM((3, reqs, 8 + drafts, hidden), F32),
            pltpu.VMEM((heads, reqs, drafts, DK), BF16),
            pltpu.VMEM((heads, reqs, drafts, DK), F32),
            pltpu.VMEM((heads, reqs, drafts, DK), F32),
            pltpu.VMEM((rows, heads), F32),
            pltpu.VMEM((rows, hidden), BF16),
            pltpu.VMEM((heads, reqs, 3 * drafts, DK), BF16),
            pltpu.VMEM((heads, reqs, 3 * drafts, DK), BF16),
            pltpu.VMEM((2, n_tp, MOVE * drafts, cols), BF16),
            pltpu.VMEM((2, n_tp, MOVE * drafts, cols), BF16),
            pltpu.VMEM(tokens.shape, BF16),
            pltpu.VMEM((reqs + 2 * MOVE, drafts, cols), BF16),
            pltpu.VMEM(state_pages.shape, BF16),
            dma((9,)),
            dma((heads,)),
            dma((heads,)),
            dma,
            dma,
            dma((2,)),
            dma((2,)),
            dma((2, n_tp)),
            dma((2, n_tp)),
            dma((2, n_tp)),
            dma((2, n_tp)),
            dma((2,)),
            dma((2,)),
        ],
        compiler_params=pltpu.CompilerParams(
            collective_id=0, has_side_effects=True, vmem_limit_bytes=60 * 1024 * 1024
        ),
    )(
        page_order,
        draft_lengths,
        accepted,
        tokens,
        gain_in,
        w_beta.T,
        jnp.transpose(conv_weight, (1, 0, 2)),
        out_gain.reshape(1, -1),
        jnp.transpose(conv_pages, (1, 2, 0, 3)),
        w_qkv,
        w_out,
        state_pages,
    )
    mixed, final_conv, pages = pl.pallas_call(
        hand_out,
        out_shape=tuple(jax.ShapeDtypeStruct(a.shape, a.dtype) for a in results),
        in_specs=[hbm] * 3,
        out_specs=(hbm,) * 3,
        scratch_shapes=[dma((reqs + 2,))],
        compiler_params=pltpu.CompilerParams(vmem_limit_bytes=60 * 1024 * 1024),
    )(*results)
    return mixed, pages, jnp.transpose(final_conv, (2, 0, 1, 3))


def solution(mesh):
    return jax.shard_map(
        functools.partial(on_device, mesh.shape["seq"], mesh.shape["tp"]),
        mesh=mesh,
        in_specs=(
            P("seq", None, "tp"),
            P(),
            P(None, None, "tp"),
            P(None, "tp"),
            P(None, None, "tp"),
            P(),
            P("tp", None),
            P("seq", "tp", None, None),
            P("seq", None, None, "tp"),
            P(),
            P(),
            P(),
        ),
        out_specs=(P("seq", None, "tp"), P("seq", "tp", None, None), P("seq", None, None, "tp")),
        check_vma=False,
    )
```

time: 46.8 us -> 115 us (2.46)
  Pallas kernels: 34.6 us -> 114 us
  local copies, waits for them, and re-layouts: 11.2 us -> 0 us
    pallas_call x0 -> x1, Pallas kernels: none -> 77.1 us  [on_device(): pl.pallas_call(hand_out, out_shape=tuple((jax.ShapeDtypeStruct(a.shape, a...]
    unnamed x19 -> x0, local copies, waits for them, and re-layouts: 10.5 us -> none
    pallas_call x1, Pallas kernels: 34.6 us -> 36.9 us  [on_device(): pl.pallas_call(functools.partial(kernel, n_seq, n_tp), out_shape=(jax.Sha...]
where the time goes in v2:
time: 115 us
  Pallas kernels  114 us (99%)
    pallas_call x1, Pallas kernels, on_device(): pl.pallas_call(hand_out, out_shape=tuple((jax.ShapeDtypeStruct(a.shape, a...  77.1 us
    pallas_call x1, Pallas kernels, on_device(): pl.pallas_call(functools.partial(kernel, n_seq, n_tp), out_shape=(jax.Sha...  36.9 us

profile of v2, /device:TPU:0, one launch (start us, length us, event | category | flops | bytes accessed | tf_op | source)
XLA Modules:
  0.0 114.7 jit_solution(13165865548377308909)
XLA Ops:
  0.6 36.9 %shard_map.139 = (bf16[8,16,1024]{2,1,0:T(8,128)(2,1)}, bf16[3,3,8,1024]{3,2,1,0:T(8,128)(2,1)}, bf16[8,8,128,128]{3,2,1,0:T(8,128)(2,1)}) custom-call(s32[128]{0:T(128)} %po_hbm.1, s32[128]{0:T(128)} %len_hbm.1, s32[128]{0:T(128)} %acc_hbm.1, bf16[8,16,1024]{2,1,0:T(8,128)(2,1)} %tok_hbm.1, bf16[2048]{0:T(1024)(128)(2,1)} %gain_hbm.1, ...), custom_call_target="tpu_custom_call" | custom-call | tf_op jit(solution)/shard_map/pallas_call | solution.py:532
  37.5 77.1 %shard_map.140 = (bf16[8,16,1024]{2,1,0:T(8,128)(2,1)}, bf16[3,3,8,1024]{3,2,1,0:T(8,128)(2,1)}, bf16[8,8,128,128]{3,2,1,0:T(8,128)(2,1)}) custom-call(bf16[8,16,1024]{2,1,0:T(8,128)(2,1)} %get-tuple-element.9.mixed_in, bf16[3,3,8,1024]{3,2,1,0:T(8,128)(2,1)} %get-tuple-element.10.fconv_in, bf16[8,8,128,128]{3,2,1,0:T(8,128)(2,1)} %get-tuple-element.11.pages_in), custom_call_target="tpu_custom_call" | custom-call | tf_op jit(solution)/shard_map/pallas_call | solution.py:603

commit v3 on v2

--- a/solution.py
+++ b/solution.py
@@ -310,7 +310,6 @@
 
     def tile(i, _):
         at = pl.ds(pl.multiple_of(i * width, width), width)
-        w_copy(i).wait()
         acts = []
         for c in range(3):
             proj = jnp.dot(normed[...], wq[c, :, at], preferred_element_type=F32)
@@ -331,7 +330,9 @@
             values[h] = acts[2][:, :, mine]
         return 0
 
-    lax.fori_loop(0, tiles, tile, 0)
+    for i in range(tiles):
+        w_copy(i).wait()
+    lax.fori_loop(0, tiles, tile, 0, unroll=True)
     st_copy.wait()
 
     def delta(side):
@@ -442,14 +443,14 @@
         done[mine] = rows_done
         back[mine] = rows_done
 
-    lax.fori_loop(0, tiles, delta(0), 0)
+    lax.fori_loop(0, tiles, delta(0), 0, unroll=True)
     wo_copy.wait()
     sums = project(0)
     second = delta(1)
     lax.fori_loop(0, 1, second, 0)
     finish(0, sums)
     returns = [to_left(done.at[pl.ds(0, MOVE)], back, ret_send, ret_recv)]
-    lax.fori_loop(1, tiles, second, 0)
+    lax.fori_loop(1, tiles, second, 0, unroll=True)
     sums = project(1)
 
     line_of = lax.broadcasted_iota(jnp.int32, (reqs, 8 + drafts, 1), 1)
@@ -491,18 +492,20 @@
     lax.fori_loop(0, heads, drain, 0)
 
 
-def hand_out(mixed_in, fconv_in, pages_in, mixed_out, fconv_out, pages_out, sem):
+def hand_out(mixed_in, fconv_in, pages_in, mixed_out, fconv_out, pages_out, *scratch):
+    mixed, fconv, pages, in_sem, out_sem = scratch
     reqs = pages_in.shape[0]
-    copies = [
-        pltpu.make_async_copy(mixed_in, mixed_out, sem.at[reqs]),
-        pltpu.make_async_copy(fconv_in, fconv_out, sem.at[reqs + 1]),
-    ]
-    for j in range(reqs):
-        copies.append(pltpu.make_async_copy(pages_in.at[j], pages_out.at[j], sem.at[j]))
-    for copy in copies:
-        copy.start()
-    for copy in copies:
-        copy.wait()
+    routes = [(pages_in.at[j], pages.at[j], pages_out.at[j]) for j in range(reqs)]
+    routes += [(mixed_in, mixed, mixed_out), (fconv_in, fconv, fconv_out)]
+    reads = [pltpu.make_async_copy(r[0], r[1], in_sem.at[i]) for i, r in enumerate(routes)]
+    writes = [pltpu.make_async_copy(r[1], r[2], out_sem.at[i]) for i, r in enumerate(routes)]
+    for read in reads:
+        read.start()
+    for read, write in zip(reads, writes):
+        read.wait()
+        write.start()
+    for write in writes:
+        write.wait()
 
 
 def on_device(
@@ -605,7 +608,8 @@
         out_shape=tuple(jax.ShapeDtypeStruct(a.shape, a.dtype) for a in results),
         in_specs=[hbm] * 3,
         out_specs=(hbm,) * 3,
-        scratch_shapes=[dma((reqs + 2,))],
+        scratch_shapes=[pltpu.VMEM(a.shape, a.dtype) for a in results]
+        + [dma((reqs + 2,)), dma((reqs + 2,))],
         compiler_params=pltpu.CompilerParams(vmem_limit_bytes=60 * 1024 * 1024),
     )(*results)
     return mixed, pages, jnp.transpose(final_conv, (2, 0, 1, 3))

time: 115 us -> 38.6 us (0.34)
  Pallas kernels: 114 us -> 37.8 us
    pallas_call x1, Pallas kernels: 77.1 us -> 2.56 us  [on_device(): pl.pallas_call(hand_out, out_shape=tuple((jax.ShapeDtypeStruct(a.shape, a...]
    pallas_call x1, Pallas kernels: 36.9 us -> 35.2 us  [on_device(): pl.pallas_call(functools.partial(kernel, n_seq, n_tp), out_shape=(jax.Sha...]
where the time goes in v3:
time: 38.6 us; the launch traced here: 38.4 us
  Pallas kernels  37.8 us (98%)
  between operations  0.64 us (2%)
    pallas_call x1, Pallas kernels, on_device(): pl.pallas_call(functools.partial(kernel, n_seq, n_tp), out_shape=(jax.Sha...  35.2 us
    pallas_call x1, Pallas kernels, on_device(): pl.pallas_call(hand_out, out_shape=tuple((jax.ShapeDtypeStruct(a.shape, a...  2.56 us

profile of v3, /device:TPU:0, one launch (start us, length us, event | category | flops | bytes accessed | tf_op | source)
XLA Modules:
  0.0 38.4 jit_solution(13664709446564293256)
XLA Ops:
  0.6 35.2 %shard_map.139 = (bf16[8,16,1024]{2,1,0:T(8,128)(2,1)}, bf16[3,3,8,1024]{3,2,1,0:T(8,128)(2,1)}, bf16[8,8,128,128]{3,2,1,0:T(8,128)(2,1)}) custom-call(s32[128]{0:T(128)} %po_hbm.1, s32[128]{0:T(128)} %len_hbm.1, s32[128]{0:T(128)} %acc_hbm.1, bf16[8,16,1024]{2,1,0:T(8,128)(2,1)} %tok_hbm.1, bf16[2048]{0:T(1024)(128)(2,1)} %gain_hbm.1, ...), custom_call_target="tpu_custom_call" | custom-call | tf_op jit(solution)/shard_map/pallas_call | solution.py:535
  35.9 2.6 %shard_map.140 = (bf16[8,16,1024]{2,1,0:T(8,128)(2,1)}, bf16[3,3,8,1024]{3,2,1,0:T(8,128)(2,1)}, bf16[8,8,128,128]{3,2,1,0:T(8,128)(2,1)}) custom-call(bf16[8,16,1024]{2,1,0:T(8,128)(2,1)} %get-tuple-element.9.mixed_in, bf16[3,3,8,1024]{3,2,1,0:T(8,128)(2,1)} %get-tuple-element.10.fconv_in, bf16[8,8,128,128]{3,2,1,0:T(8,128)(2,1)} %get-tuple-element.11.pages_in), custom_call_target="tpu_custom_call" | custom-call | tf_op jit(solution)/shard_map/pallas_call | solution.py:606

commit v4 on v3

--- a/solution.py
+++ b/solution.py
@@ -464,7 +464,6 @@
             ).astype(BF16)
         return 0
 
-    lax.fori_loop(0, 3, edges, 0)
     finish(1, sums)
     returns.append(to_right(done.at[pl.ds(MOVE, MOVE)], back, ret_send, ret_recv))
 
@@ -485,6 +484,7 @@
         return 0
 
     lax.fori_loop(0, heads, accept, 0)
+    lax.fori_loop(0, 3, edges, 0)
     for copy in returns:
         copy.wait()
     for i in range(reqs):

time: 38.6 us -> 37.6 us (0.974)
  Pallas kernels: 37.8 us -> 36.8 us
    pallas_call x1, Pallas kernels: 35.2 us -> 34.2 us  [on_device(): pl.pallas_call(functools.partial(kernel, n_seq, n_tp), out_shape=(jax.Sha...]
where the time goes in v4:
time: 37.6 us; the launch traced here: 37.4 us
  Pallas kernels  36.8 us (98%)
  between operations  0.64 us (2%)
    pallas_call x1, Pallas kernels, on_device(): pl.pallas_call(functools.partial(kernel, n_seq, n_tp), out_shape=(jax.Sha...  34.2 us
    pallas_call x1, Pallas kernels, on_device(): pl.pallas_call(hand_out, out_shape=tuple((jax.ShapeDtypeStruct(a.shape, a...  2.56 us

profile of v4, /device:TPU:0, one launch (start us, length us, event | category | flops | bytes accessed | tf_op | source)
XLA Modules:
  0.0 37.4 jit_solution(18360842484153322794)
XLA Ops:
  0.6 34.2 %shard_map.139 = (bf16[8,16,1024]{2,1,0:T(8,128)(2,1)}, bf16[3,3,8,1024]{3,2,1,0:T(8,128)(2,1)}, bf16[8,8,128,128]{3,2,1,0:T(8,128)(2,1)}) custom-call(s32[128]{0:T(128)} %po_hbm.1, s32[128]{0:T(128)} %len_hbm.1, s32[128]{0:T(128)} %acc_hbm.1, bf16[8,16,1024]{2,1,0:T(8,128)(2,1)} %tok_hbm.1, bf16[2048]{0:T(1024)(128)(2,1)} %gain_hbm.1, ...), custom_call_target="tpu_custom_call" | custom-call | tf_op jit(solution)/shard_map/pallas_call | solution.py:535
  34.8 2.6 %shard_map.140 = (bf16[8,16,1024]{2,1,0:T(8,128)(2,1)}, bf16[3,3,8,1024]{3,2,1,0:T(8,128)(2,1)}, bf16[8,8,128,128]{3,2,1,0:T(8,128)(2,1)}) custom-call(bf16[8,16,1024]{2,1,0:T(8,128)(2,1)} %get-tuple-element.9.mixed_in, bf16[3,3,8,1024]{3,2,1,0:T(8,128)(2,1)} %get-tuple-element.10.fconv_in, bf16[8,8,128,128]{3,2,1,0:T(8,128)(2,1)} %get-tuple-element.11.pages_in), custom_call_target="tpu_custom_call" | custom-call | tf_op jit(solution)/shard_map/pallas_call | solution.py:606
